TPU v7x, 512 devices: a whole 4x8x8 slice. The times are simulated.
512 devices in a mesh: dp: 16 (over x_lo, y), vocab: 32 (over x_hi, z, core).
Axes of the slice: x: 4 (x_hi: 2, x_lo: 2; x = x_hi * 2 + x_lo), y: 8, z: 8, core: 2. Of those that a mesh axis runs over, the one named last changes fastest.
Arguments:
- teacher_hidden: bfloat16 [384, 4608], P('dp', 'vocab'), may hold values from -6 to 6
- teacher_head: bfloat16 [4608, 131072], P(None, ('dp', 'vocab')), may hold values from -0.625 to 0.625
- student_hidden: bfloat16 [384, 2304], P('dp', 'vocab'), may hold values from -6 to 6
- student_gain: float32 [2304], replicated, may hold values from 0.5 to 1.5
- student_head: bfloat16 [2304, 131072], P(None, ('dp', 'vocab')), may hold values from -1 to 1
- token_mask: int32 [384], replicated, may hold values 0 or 1
Outputs:
- token_kl: float32 [384], replicated
- loss: float32 [], replicated
- grad_hidden: float32 [384, 2304], P('dp', 'vocab')
- grad_gain: float32 [2304], P('vocab')
All inputs are finite; a program needn't handle non-finite values.
Results may differ from a plain program's by a relative error of at most 0.0053.
Values may be sent and summed in bfloat16 or wider, within the bound.
A program may use at most 64 MiB of HBM per device.

v0:
```python
import jax
import jax.numpy as jnp
from jax import lax
from jax.sharding import PartitionSpec as P


def on_device(teacher_hidden, teacher_head, student_hidden, student_gain, student_head, token_mask):
    local_cols = student_hidden.shape[1]
    full_width = local_cols * lax.axis_size("vocab")
    start_col = lax.axis_index("vocab") * local_cols
    gain_local = lax.dynamic_slice_in_dim(student_gain, start_col, local_cols, 0)
    xlocal = student_hidden.astype(jnp.float32)
    squares = lax.psum(jnp.sum(xlocal * xlocal, axis=1), "vocab")
    scale_local = lax.rsqrt(squares / full_width + 1e-06)
    student_piece = (xlocal * scale_local[:, None] * gain_local[None, :]).astype(jnp.bfloat16)
    wide_t, wide_s = (
        lax.all_gather(teacher_hidden, "vocab", axis=1, tiled=True),
        lax.all_gather(student_piece, "vocab", axis=1, tiled=True),
    )
    teacher_rows, student_rows = (
        lax.all_gather(wide_t, "dp", axis=0, tiled=True),
        lax.all_gather(wide_s, "dp", axis=0, tiled=True),
    )
    teach = 30.0 * jnp.tanh(
        jnp.dot(teacher_rows, teacher_head, preferred_element_type=jnp.float32) / 30.0
    )
    pupil = 30.0 * jnp.tanh(
        jnp.dot(student_rows, student_head, preferred_element_type=jnp.float32) / 30.0
    )
    exp_teach = jnp.exp(teach - 30.0)
    exp_pupil = jnp.exp(pupil - 30.0)
    total_teach, total_pupil, cross = lax.psum(
        (
            jnp.sum(exp_teach, axis=1),
            jnp.sum(exp_pupil, axis=1),
            jnp.sum(exp_teach * (teach - pupil), axis=1),
        ),
        ("dp", "vocab"),
    )
    token_kl = cross / total_teach - jnp.log(total_teach) + jnp.log(total_pupil)
    maskf = token_mask.astype(jnp.float32)
    weight = maskf / jnp.maximum(jnp.sum(maskf), 1.0)
    loss = jnp.sum(weight * token_kl)
    dpupil = weight[:, None] * (exp_pupil / total_pupil[:, None] - exp_teach / total_teach[:, None])
    dpupil = (dpupil * (1.0 - (pupil / 30.0) ** 2)).astype(jnp.bfloat16)
    partial_grad = lax.dot_general(
        dpupil, student_head, (((1,), (1,)), ((), ())), preferred_element_type=jnp.float32
    )
    column_sum = lax.psum_scatter(partial_grad, "vocab", scatter_dimension=1, tiled=True)
    dnormed = lax.psum_scatter(column_sum, "dp", scatter_dimension=0, tiled=True)
    rowdot = lax.psum(jnp.sum(dnormed * gain_local[None, :] * xlocal, axis=1), "vocab")
    grad_hidden = (
        gain_local[None, :] * dnormed * scale_local[:, None]
        - xlocal * (scale_local**3 * rowdot / full_width)[:, None]
    )
    grad_gain = lax.psum(jnp.sum(dnormed * xlocal * scale_local[:, None], axis=0), "dp")
    return (token_kl, loss, grad_hidden, grad_gain)


def solution(mesh):
    placed = (
        P("dp", "vocab"),
        P(None, ("dp", "vocab")),
        P("dp", "vocab"),
        P(),
        P(None, ("dp", "vocab")),
        P(),
    )
    return jax.shard_map(
        on_device,
        mesh=mesh,
        in_specs=placed,
        out_specs=(P(), P(), P("dp", "vocab"), P("vocab")),
        check_vma=False,
    )
```

profile of v0, /device:TPU:4, one launch (start us, length us, event | category | flops | bytes accessed | tf_op | source)
XLA Modules:
  0.0 751.4 jit_solution(15646408305311245896)
XLA Ops:
  7.3 1.0 fusion.12
  8.2 73.6 %psum.42 = f32[24]{0:T(128)S(1)} all-reduce(f32[24]{0:T(128)S(1)} %fusion.12), channel_id=1, replica_groups=mesh['dp'=16,'vocab'=32] {'vocab'}, use_global_device_ids=true, to_apply=%region_1.0 | all-reduce | flops 24 | bytes 192 | tf_op jit(solution)/shard_map/psum | solution.py:13
  81.8 0.8 dynamic_slice.3
  83.1 0.8 fusion.19
  83.9 36.9 %all-gather.1 = bf16[32,72,24]{1,2,0:T(8,128)(2,1)S(1)} all-gather(bf16[1,72,24]{1,2,0:T(8,128)(2,1)S(1)} %fusion.19), channel_id=1, replica_groups=mesh['dp'=16,'vocab'=32] {'vocab'}, dimensions={0}, use_global_device_ids=true | all-gather | bytes 114048 | tf_op jit(solution)/shard_map/all_gather | solution.py:18
  120.8 0.7 copy.19
  121.5 1.9 reshape.17
  123.4 39.9 %all-gather = bf16[32,144,24]{1,2,0:T(8,128)(2,1)S(1)} all-gather(bf16[1,144,24]{1,2,0:T(8,128)(2,1)} %bitcast.24), channel_id=1, replica_groups=mesh['dp'=16,'vocab'=32] {'vocab'}, dimensions={0}, use_global_device_ids=true | all-gather | bytes 228096 | tf_op jit(solution)/shard_map/all_gather | solution.py:17
  163.3 0.8 copy.18
  164.1 2.2 reshape.15
  167.6 27.0 %all-gather.7.cloned.1.call-done = bf16[384,2304]{1,0:T(8,128)(2,1)} async-done(((bf16[24,2304]{1,0:T(8,128)(2,1)}), bf16[384,2304]{1,0:T(8,128)(2,1)}) %all-gather.7.cloned.1.call-update) | async-done | bytes 1769488 | tf_op jit(solution)/shard_map/all_gather | solution.py:22
  194.6 3.1 fusion.2
  197.7 75.3 %all-gather.5.cloned.1.call-done = bf16[384,4608]{1,0:T(8,128)(2,1)} async-done(((bf16[24,4608]{1,0:T(8,128)(2,1)}), bf16[384,4608]{1,0:T(8,128)(2,1)}) %all-gather.5.cloned.1.call-update) | async-done | bytes 3538960 | tf_op jit(solution)/shard_map/all_gather | solution.py:21
  272.9 4.9 multiply_reduce_fusion
  277.9 95.4 %all-reduce.2 = (f32[384]{0:T(512)S(1)}, f32[384]{0:T(512)S(1)}, f32[384]{0:T(512)}) all-reduce(f32[384]{0:T(512)} %get-tuple-element.13, f32[384]{0:T(512)} %get-tuple-element.14, f32[384]{0:T(512)} %get-tuple-element.12), channel_id=1, replica_groups=mesh['dp'=16,'vocab'=32] {'dp','vocab'}, use_global_device_ids=true, to_apply=%region_7.0 | all-reduce | flops 1152 | bytes 9216 | tf_op jit(solution)/shard_map/psum | solution.py:32
  373.3 1.9 multiply_reduce_fusion.1
  375.1 3.8 fusion.5
  379.0 129.0 %reduce-scatter.5.cloned.1.call-done = f32[384,72]{0,1:T(8,128)} async-done(((f32[384,2304]{0,1:T(8,128)}), f32[384,72]{0,1:T(8,128)}) %reduce-scatter.5.cloned.1.call-update) | async-done | bytes 110608
  508.1 1.3 dynamic-slice.2
  510.0 136.2 %all-reduce.5.cloned.1.call-done = f32[384,72]{0,1:T(8,128)} async-done(((f32[384,72]{0,1:T(8,128)}), f32[384,72]{0,1:T(8,128)}) %all-reduce.5.cloned.1.call-update) | async-done | bytes 110608
  646.1 1.0 constant_dynamic-slice_fusion
  647.3 65.0 %psum.46 = f32[24]{0:T(128)S(1)} all-reduce(f32[24]{0:T(128)S(1)} %get-tuple-element.16), channel_id=1, replica_groups=mesh['dp'=16,'vocab'=32] {'vocab'}, use_global_device_ids=true, to_apply=%region_13.0 | all-reduce | flops 24 | bytes 192 | tf_op jit(solution)/shard_map/psum | solution.py:51
  712.3 0.7 fusion.16
  713.0 31.9 %psum.47 = f32[72]{0:T(128)} all-reduce(f32[72]{0:T(128)S(1)} %get-tuple-element.15), channel_id=1, replica_groups=mesh['dp'=16,'vocab'=32] {'dp'}, use_global_device_ids=true, to_apply=%region_15.0 | all-reduce | flops 72 | bytes 576 | tf_op jit(solution)/shard_map/psum | solution.py:56
  (29 shorter events, 1.6 us)
Async XLA Ops:
  7.2 265.8 %copy-start = (bf16[4608,256]{1,0:T(8,128)(2,1)S(1)}, bf16[4608,256]{1,0:T(8,128)(2,1)}, u32[]{:S(2)}) copy-start(bf16[4608,256]{1,0:T(8,128)(2,1)} %param.7) | copy-start | bytes 7077892
  7.2 159.2 %copy-start.3 = (s32[384]{0:T(512)S(1)}, s32[384]{0:T(512)}, u32[]{:S(2)}) copy-start(s32[384]{0:T(512)} %param.11) | copy-start | bytes 4612
  7.2 187.4 %copy-start.1 = (bf16[2304,256]{1,0:T(8,128)(2,1)S(1)}, bf16[2304,256]{1,0:T(8,128)(2,1)}, u32[]{:S(2)}) copy-start(bf16[2304,256]{1,0:T(8,128)(2,1)} %param.10) | copy-start | bytes 3538948
  7.2 187.4 %all-gather.7.cloned.1.call-start = ((), (), s32[]{:S(2)}) async-start(), calls=%async_computation.2 | async-start | bytes 1880064 | tf_op jit(solution)/shard_map/all_gather | solution.py:22
  81.8 115.9 %copy-start.6 = (f32[24]{0:T(128)}, f32[24]{0:T(128)S(1)}, u32[]{:S(2)}) copy-start(f32[24]{0:T(128)S(1)} %psum.42) | copy-start | bytes 292
  82.6 0.5 copy-start.4
  123.4 149.6 %all-gather.5.cloned.1.call-start = ((), (), s32[]{:S(2)}) async-start(), calls=%async_computation.1 | async-start | bytes 3760128 | tf_op jit(solution)/shard_map/all_gather | solution.py:21
  166.3 341.7 %reduce-scatter.5.cloned.1.call-start = ((), (), s32[]{:S(2)}) async-start(), calls=%async_computation.4 | async-start | bytes 3649536
  378.9 268.2 %copy-start.2 = (bf16[24,72]{1,0:T(8,128)(2,1)S(1)}, bf16[24,72]{1,0:T(8,128)(2,1)}, u32[]{:S(2)}) copy-start(bf16[24,72]{1,0:T(8,128)(2,1)} %param.8) | copy-start | bytes 10372
  378.9 268.2 %copy-start.5 = (f32[72]{0:T(128)S(1)}, f32[72]{0:T(128)}, u32[]{:S(2)}) copy-start(f32[72]{0:T(128)} %copy-done.4) | copy-start | bytes 868
  378.9 333.4 %copy-start.7 = (f32[24]{0:T(128)S(1)}, f32[24]{0:T(128)}, u32[]{:S(2)}) copy-start(f32[24]{0:T(128)} %copy-done.6) | copy-start | bytes 292
  379.0 267.2 %all-reduce.5.cloned.1.call-start = ((), (), s32[]{:S(2)}) async-start(), calls=%async_computation.3 | async-start | bytes 221184
Sparse Core Ops, SparseCore 0:
  123.5 71.1 all-gather.6
  196.7 76.1 all-gather.4
  379.1 128.9 reduce-scatter.4
  510.8 135.2 all-reduce.4
where the time goes:
time: 752 us; the launch traced here: 751 us
  waiting for transfers between devices  368 us (49%)
  blocking collectives  343 us (46%)
  between operations  15.1 us (2%)
  matrix products  11.8 us (2%)
  local copies, waits for them, and re-layouts  9.22 us (1%)
    unnamed x6, waiting for transfers between devices  265 us
    psum x1, blocking collectives, on_device(): lax.psum((jnp.sum(exp_teach, axis=1), jnp.sum(exp_pupil, axis=1), jnp.sum...  95.4 us
    all_gather x1, waiting for transfers between devices, on_device(): lax.all_gather(wide_t, 'dp', axis=0, tiled=True)  75.3 us
    psum x1, blocking collectives, on_device(): squares = lax.psum(jnp.sum(xlocal * xlocal, axis=1), 'vocab')  73.6 us
    psum x1, blocking collectives, on_device(): lax.psum(jnp.sum(dnormed * gain_local[None, :] * xlocal, axis=1), 'vocab')  65 us
    all_gather x1, blocking collectives, on_device(): lax.all_gather(teacher_hidden, 'vocab', axis=1, tiled=True)  39.9 us
    all_gather x1, blocking collectives, on_device(): lax.all_gather(student_piece, 'vocab', axis=1, tiled=True)  36.9 us
    psum x1, blocking collectives, on_device(): lax.psum(jnp.sum(dnormed * xlocal * scale_local[:, None], axis=0), 'dp')  31.9 us
  transfers between devices with their start and end apart: 4, of which 4 were waited for; matrix products, arithmetic and copies ran while one was open for 1% of the time, Pallas kernels for 0%

commit v1 on v0

v1 whole, which is shorter than its diff:
```python
import jax
import jax.numpy as jnp
from jax import lax
from jax.experimental import pallas as pl
from jax.experimental.pallas import tpu as pltpu
from jax.sharding import PartitionSpec as P

F32, BF16 = jnp.float32, jnp.bfloat16
MESH = pl.DeviceIdType.MESH
N = 8
TOK, ROWS = 384, 24
TF, SF = 144, 72
SP = 80
VOC = 256
STOP = 99


def body(
    th, sh, gain, mask, wt_hbm, ws_hbm,
    kl_out, loss_out, gh_out, gg_out,
    wt, ws, wtt, wst, wsr, gb, pad_t, pad_s, piece, got, xt, xs, ns,
    ls, lt, pu, ep, qq, ql, et, dpu, s_own, s_sib, s_z, s_y, s_x, cols,
    g_own, g_out, g_in, r_out, r_in, e_out, e_in, f_out, f_in,
    w_sem, p_send, p_recv, h_send, h_recv, ring_send, ring_recv, sib_send, sib_recv,
    a_send, a_recv, z_send, z_recv, y_send, y_recv, x_send, x_recv,
    gs_send, gs_recv, rr_send, rr_recv, e_send, e_recv, f_send, f_recv,
):
    d, v = lax.axis_index("dp"), lax.axis_index("vocab")
    xl, y = d // N, d % N
    s, z, xh = v % 2, (v // 2) % N, v // (2 * N)
    first = s == 0
    p = jnp.where(first, z, y)
    q = jnp.where(first, y, z)

    def dev(xl, y, xh, z, s):
        return (xl * N + y, (xh * N + z) * 2 + s)

    def ring(place):
        return dev(xl, jnp.where(first, y, place), xh, jnp.where(first, place, z), s)

    def holder(m):
        a, j = m // N, m % N
        return dev(a, jnp.where(first, j, z), xh, jnp.where(first, z, j), s)

    def owner(m):
        return dev(m // N, m % N, xh, p, s)

    self_in = jnp.logical_or(first, y == z)
    right, left = ring((p + 1) % N), ring((p + N - 1) % N)
    sibling = dev(xl, y, xh, z, 1 - s)
    across = dev(1 - xl, y, 1 - xh, z, s)

    def remote(src, dst, send, recv, to):
        return pltpu.make_async_remote_copy(
            src_ref=src, dst_ref=dst, send_sem=send, recv_sem=recv, device_id=to, device_id_type=MESH
        )

    wt_copy = pltpu.make_async_copy(wt_hbm, wt, w_sem.at[0])
    ws_copy = pltpu.make_async_copy(ws_hbm, ws, w_sem.at[1])
    wt_copy.start()
    ws_copy.start()

    barrier = pltpu.get_barrier_semaphore()

    def tell(to):
        pl.semaphore_signal(barrier, inc=1, device_id=to, device_id_type=MESH)

    def greet(m, _):
        for who in (holder(m), owner(m)):
            @pl.when(jnp.logical_not(jnp.logical_and(who[0] == d, who[1] == v)))
            def _():
                tell(who)
        return 0

    lax.fori_loop(0, 2 * N, greet, 0)

    def greet_lines(j, _):
        tell(dev(xl, y, xh, (z + j) % N, s))
        tell(dev(xl, (y + j) % N, xh, z, s))
        return 0

    lax.fori_loop(1, N, greet_lines, 0)
    tell(sibling)
    for a, b in ((1 - xl, xh), (xl, 1 - xh), (1 - xl, 1 - xh)):
        tell(dev(a, y, b, z, s))

    pad_t[...] = jnp.zeros_like(pad_t)
    pad_s[...] = jnp.zeros_like(pad_s)
    pad_t[:, :TF] = th[...].astype(F32)
    pad_s[:, :SF] = sh[...].astype(F32)
    lane = lax.broadcasted_iota(jnp.int32, (ROWS, 128), 1)
    low = jnp.where(lane < TF - 128, pad_t[:, 128:256], pltpu.roll(pad_s[...], TF - 128, 1))
    piece[...] = jnp.concatenate([pad_t[:, :128], low], axis=0).astype(BF16)

    @pl.when(self_in)
    def _():
        got[d] = piece[...]

    pl.semaphore_wait(barrier, 4 * N - 2 * self_in.astype(jnp.int32) + 2 * (N - 1) + 4)

    def piece_send(m):
        return remote(piece, got.at[d], p_send.at[m], p_recv.at[d], holder(m))

    def away(m):
        who = holder(m)
        return jnp.logical_not(jnp.logical_and(who[0] == d, who[1] == v))

    def send_pieces(i, _):
        m = (d + 1 + i) % (2 * N)

        @pl.when(away(m))
        def _():
            piece_send(m).start()

        return 0

    lax.fori_loop(0, 2 * N, send_pieces, 0)

    for i in range(18):
        gb[i * 128:(i + 1) * 128, :] = jnp.broadcast_to(gain[i:i + 1, :], (128, 128)).T
    ws_copy.wait()

    def reorder(c, _):
        one = ws[pl.ds(pl.multiple_of(c * TF, 16), TF), :].astype(F32)
        two = ws[pl.ds(pl.multiple_of((N + c) * TF, 16), TF), :].astype(F32)
        wsr[c] = jnp.concatenate([one[:SF], two[:SF]], axis=0).astype(BF16)
        wsr[N + c] = jnp.concatenate([one[SF:], two[SF:]], axis=0).astype(BF16)
        return 0

    lax.fori_loop(0, N, reorder, 0)

    def turn_student(i):
        block = wsr[i * N:(i + 1) * N].reshape(N * TF, VOC)
        for j in range(9):
            wst[i, :, j * 128:(j + 1) * 128] = block[j * 128:(j + 1) * 128, :].T

    def turn_teacher(i):
        for j in range(9):
            at = (i * 9 + j) * 128
            wtt[i, :, j * 128:(j + 1) * 128] = wt[at:at + 128, :].T

    turn_student(0)
    turn_student(1)

    def wait_pieces(m, _):
        @pl.when(jnp.logical_not(jnp.logical_and(self_in, m == d)))
        def _():
            remote(piece, got.at[m], p_send.at[m], p_recv.at[m], sibling).wait_recv()

        return 0

    lax.fori_loop(0, 2 * N, wait_pieces, 0)

    pieces = [got[m].astype(F32) for m in range(2 * N)]
    upper = jnp.concatenate([t[:ROWS] for t in pieces], axis=0).T
    lower = jnp.concatenate([t[ROWS:] for t in pieces], axis=0).T
    tail = TF - 128
    mine_t, mine_s = (xh * N + p) * 2 + s, s * 2 * N + xh * N + p
    xt[mine_t] = jnp.concatenate([upper, lower[:tail]], axis=0).astype(BF16)
    xs[mine_s] = lower[tail:tail + SP].astype(BF16)

    def unit(core, place, other, teacher):
        half = 1 - xh if other else xh
        if teacher:
            return xt.at[(half * N + place) * 2 + core]
        return xs.at[core * 2 * N + half * N + place]

    sent = []

    def push(ref, send, recv, to):
        copy = remote(ref, ref, send, recv, to)
        copy.start()
        sent.append(copy)

    for kind in (0, 1):
        push(unit(s, p, 0, kind), h_send.at[kind], h_recv.at[kind], across)

    units = [(0, 0), (0, 1), (1, 0), (1, 1)]

    def to_ring(way, step, u, place):
        i = (way * 4 + step) * 4 + u
        push(unit(s, place, *units[u]), ring_send.at[i], ring_recv.at[i], (right, left)[way])

    def from_ring(way, step, u, place):
        i = (way * 4 + step) * 4 + u
        ref = unit(s, place, *units[u])
        remote(ref, ref, ring_send.at[i], ring_recv.at[i], sibling).wait_recv()

    def to_sibling(slot, u, place):
        i = slot * 4 + u
        push(unit(s, place, *units[u]), sib_send.at[i], sib_recv.at[i], sibling)

    def from_sibling(slot, u, place):
        i = slot * 4 + u
        ref = unit(1 - s, place, *units[u])
        remote(ref, ref, sib_send.at[i], sib_recv.at[i], sibling).wait_recv()

    def behind(place, way, step):
        return (place + (N - step if way == 0 else step)) % N

    for u, (other, kind) in enumerate(units):
        if other:
            ref = unit(s, p, other, kind)
            remote(ref, ref, h_send.at[kind], h_recv.at[kind], sibling).wait_recv()
        to_ring(0, 0, u, p)
        to_ring(1, 0, u, p)
        to_sibling(0, u, p)
        if u == 0:
            wt_copy.wait()
            turn_teacher(0)
    turn_teacher(1)

    for step in (1, 2, 3):
        for u, (other, kind) in enumerate(units):
            for way in (0, 1):
                place = behind(p, way, step)
                from_ring(way, step - 1, u, place)
                if step < 3 or other == way:
                    to_ring(way, step, u, place)
                to_sibling(way * 3 + step, u, place)
        if step < 3:
            turn_teacher(step + 1)

    far, sib_far = behind(p, 0, 4), behind(q, 0, 4)

    def last(kind):
        for way in (0, 1):
            u = units.index((way, kind))
            from_ring(way, 3, u, far)
            to_sibling(7, u, far)

    def all_from_sibling(kind):
        for other in (0, 1):
            u = units.index((other, kind))
            from_sibling(0, u, q)
            for step in (1, 2, 3):
                for way in (0, 1):
                    from_sibling(way * 3 + step, u, behind(q, way, step))
            from_sibling(7, u, sib_far)

    last(0)
    all_from_sibling(0)

    def squares(i, total):
        x = xs[i].astype(F32)
        for j in range(SF // 8):
            part = x[j * 8:(j + 1) * 8]
            total = total + part * part
        return total

    total = lax.fori_loop(0, 4 * N, squares, jnp.zeros((8, TOK), F32))
    scale = lax.rsqrt(jnp.sum(total, axis=0, keepdims=True) / (SF * 4 * N) + 1e-6)

    def normalise(i, _):
        core, c = i // N, i % N
        base = core * 2 * N + c
        for half in (0, 1):
            x = xs[base + half * N].astype(F32)[:SF]
            at = pl.multiple_of(((half * N + c) * 2 + core) * SF, 8)
            g = gb[pl.ds(at, SF), :]
            n = (x * scale) * jnp.concatenate([g, g, g], axis=1)
            if half == 0:
                head = n
        ns[i] = jnp.concatenate([head, n], axis=0).astype(BF16)
        return 0

    lax.fori_loop(0, 2 * N, normalise, 0)

    def dot(a, b):
        return jnp.dot(a, b, preferred_element_type=F32)

    ls[...] = dot(wst[0], ns[0:N].reshape(N * TF, TOK))
    ls[...] += dot(wst[1], ns[N:2 * N].reshape(N * TF, TOK))

    step_rows = 32

    def fold(x):
        out = x[0:8]
        for j in range(1, step_rows // 8):
            out = out + x[j * 8:(j + 1) * 8]
        return out

    zero = jnp.zeros((8, TOK), F32)

    def student(i, carry):
        at = pl.ds(pl.multiple_of(i * step_rows, step_rows), step_rows)
        logit = ls[at, :]
        pupil = 30.0 * jnp.tanh(logit / 30.0)
        e = jnp.exp(pupil - 30.0)
        slope = 1.0 - (pupil / 30.0) ** 2
        pu[at, :], ep[at, :], qq[at, :] = pupil, e, slope
        sl = slope * logit
        ql[at, :] = sl
        return carry[0] + fold(e), carry[1] + fold(e * sl)

    zs8, u8 = lax.fori_loop(0, VOC // step_rows, student, (zero, zero))

    last(1)
    all_from_sibling(1)

    def teacher_dot(i, _):
        b = xt[pl.ds(i * N, N)].reshape(N * TF, TOK)
        lt[...] += dot(wtt[i], b)
        return 0

    lt[...] = jnp.zeros_like(lt)
    lax.fori_loop(0, 4, teacher_dot, 0)

    def teacher(i, carry):
        at = pl.ds(pl.multiple_of(i * step_rows, step_rows), step_rows)
        teach = 30.0 * jnp.tanh(lt[at, :] / 30.0)
        e = jnp.exp(teach - 30.0)
        et[at, :] = e
        return (
            carry[0] + fold(e),
            carry[1] + fold(e * (teach - pu[at, :])),
            carry[2] + fold(e * ql[at, :]),
        )

    zt8, c8, v8 = lax.fori_loop(0, VOC // step_rows, teacher, (zero, zero, zero))
    five = [jnp.sum(t, axis=0, keepdims=True) for t in (zt8, zs8, c8, u8, v8)]
    s_own[...] = jnp.concatenate(five + [jnp.zeros((3, TOK), F32)], axis=0)

    push_sums = remote(s_own, s_sib, a_send.at[0], a_recv.at[0], sibling)
    push_sums.start()
    push_sums.wait_recv()
    sent.append(push_sums)
    value = s_own[...] + s_sib[...]

    def line(buf, send, recv, here, who, value):
        buf[here] = value
        for j in range(1, N):
            copy = remote(buf.at[here], buf.at[here], send.at[j], recv.at[j], who((here + j) % N))
            copy.start()
            sent.append(copy)
        for j in range(1, N):
            at = (here + N - j) % N
            remote(buf.at[at], buf.at[at], send.at[j], recv.at[j], sibling).wait_recv()
        out = buf[0]
        for j in range(1, N):
            out = out + buf[j]
        return out

    value = line(s_z, z_send, z_recv, z, lambda t: dev(xl, y, xh, t, s), value)
    value = line(s_y, y_send, y_recv, y, lambda t: dev(xl, t, xh, z, s), value)
    here = xh * 2 + xl
    s_x[here] = value
    for j, (a, b) in enumerate(((1 - xl, xh), (xl, 1 - xh), (1 - xl, 1 - xh))):
        copy = remote(s_x.at[here], s_x.at[here], x_send.at[j], x_recv.at[j], dev(a, y, b, z, s))
        copy.start()
        sent.append(copy)
    for j, (a, b) in enumerate(((1 - xl, xh), (xl, 1 - xh), (1 - xl, 1 - xh))):
        at = b * 2 + a
        remote(s_x.at[at], s_x.at[at], x_send.at[j], x_recv.at[j], sibling).wait_recv()
    value = s_x[0] + s_x[1] + s_x[2] + s_x[3]
    zt, zs, cross, us, vs = (value[i:i + 1] for i in range(5))

    maskf = mask[...].astype(F32)
    weight = maskf / jnp.maximum(jnp.sum(maskf, axis=1, keepdims=True), 1.0)
    token_kl = cross / zt - jnp.log(zt) + jnp.log(zs)
    over_s, over_t = weight / zs, weight / zt

    def gradient(i, _):
        at = pl.ds(pl.multiple_of(i * step_rows, step_rows), step_rows)
        dpu[at, :] = ((ep[at, :] * over_s - et[at, :] * over_t) * qq[at, :]).astype(BF16)
        return 0

    lax.fori_loop(0, VOC // step_rows, gradient, 0)

    offsets = (4, 3, -3, 2, -2, 1, -1, 0)
    for i, off in enumerate(offsets):
        theirs = (1 - s) * N + (q + off + N) % N
        g_out[i] = dot(wsr[theirs], dpu[...]).astype(BF16)
        copy = remote(g_out.at[i], g_in.at[i], gs_send.at[i], gs_recv.at[i], sibling)
        copy.start()
        sent.append(copy)
        g_own[i] = dot(wsr[s * N + (p + off + N) % N], dpu[...])

    kl_out[...] = token_kl
    loss_out[...] = jnp.sum(weight * token_kl, axis=1, keepdims=True)
    rowdot = (us * over_s - vs * over_t) / scale
    stacked = jnp.concatenate([scale, rowdot, jnp.zeros((126, TOK), F32)], axis=0)
    cols[...] = stacked.T

    def own(i):
        remote(g_out.at[i], g_in.at[i], gs_send.at[i], gs_recv.at[i], sibling).wait_recv()
        return g_own[i] + g_in[i].astype(F32)

    cut = (0, SP), (SP, 2 * SF)

    def hop(way, step, whole, value):
        i = way * 4 + step
        lo, hi = (0, 2 * SF) if whole else cut[way]
        r_out[i, lo:hi, :] = value.astype(BF16)
        copy = remote(
            r_out.at[i, lo:hi], r_in.at[i, lo:hi], rr_send.at[i], rr_recv.at[i], (right, left)[way]
        )
        copy.start()
        sent.append(copy)

    def arrive(way, step, whole):
        i = way * 4 + step
        lo, hi = (0, 2 * SF) if whole else cut[way]
        remote(
            r_out.at[i, lo:hi], r_in.at[i, lo:hi], rr_send.at[i], rr_recv.at[i], sibling
        ).wait_recv()
        return r_in[i, lo:hi, :].astype(F32)

    mine = own(0)
    hop(0, 0, False, mine[:SP])
    hop(1, 0, False, mine[SP:])
    mine = own(1)
    hop(0, 1, True, jnp.concatenate([mine[:SP] + arrive(0, 0, False), mine[SP:]], axis=0))
    mine = own(2)
    hop(1, 1, True, jnp.concatenate([mine[:SP], mine[SP:] + arrive(1, 0, False)], axis=0))
    for step in (2, 3):
        for way in (0, 1):
            mine = own(2 * step - 1 + way)
            hop(way, step, True, mine + arrive(way, step - 1, True))
    mine = own(7)
    g_own[0] = mine + arrive(0, 3, True) + arrive(1, 3, True)

    give = g_own[0, pl.ds(pl.multiple_of((1 - xh) * SF, 8), SF), :]
    e_out[...] = jnp.concatenate([give, jnp.zeros((SP - SF, TOK), F32)], axis=0).astype(BF16)
    copy = remote(e_out, e_in, e_send.at[0], e_recv.at[0], across)
    copy.start()
    sent.append(copy)
    keep = g_own[0, pl.ds(pl.multiple_of(xh * SF, 8), SF), :]
    x_held = xs[mine_s].astype(F32)[:SF] * scale
    gains = gb[pl.ds(pl.multiple_of(v * SF, 8), SF), :]
    filler = jnp.zeros((128 - SF, 128), F32)
    gain_row = jnp.concatenate([gains, filler], axis=0).T[:ROWS]
    mycols = cols[pl.ds(pl.multiple_of(d * ROWS, 8), ROWS), :]
    my_scale, my_rowdot = mycols[:, 0:1], mycols[:, 1:2]
    copy.wait_recv()
    keep = keep + e_in[...].astype(F32)[:SF]
    gain_grad = jnp.sum(keep * x_held, axis=1, keepdims=True)
    gain_grad = jnp.concatenate([jnp.broadcast_to(gain_grad, (SF, 128)), filler], axis=0).T[:8]
    rough = gain_grad.astype(BF16).astype(F32)
    row = lax.broadcasted_iota(jnp.int32, (8, 128), 0)
    gain_grad = jnp.where(row == 0, rough, gain_grad - rough)
    keep = jnp.concatenate([keep, jnp.zeros((128 - SF, TOK), F32)], axis=0).T
    for m in range(2 * N):
        f_out[m] = jnp.concatenate([keep[m * ROWS:(m + 1) * ROWS], gain_grad], axis=0).astype(BF16)
    slot = xl * N + q

    def final_send(m):
        return remote(f_out.at[m], f_in.at[slot], f_send.at[m], f_recv.at[slot], owner(m))

    def is_other(m):
        who = owner(m)
        return jnp.logical_not(jnp.logical_and(who[0] == d, who[1] == v))

    def send_final(i, _):
        m = (d + 1 + i) % (2 * N)

        @pl.when(is_other(m))
        def _():
            final_send(m).start()

        return 0

    lax.fori_loop(0, 2 * N, send_final, 0)

    @pl.when(self_in)
    def _():
        f_in[slot] = f_out[d]

    def wait_final(m, _):
        @pl.when(jnp.logical_not(jnp.logical_and(self_in, m == slot)))
        def _():
            remote(f_out.at[m], f_in.at[m], f_send.at[m], f_recv.at[m], sibling).wait_recv()

        return 0

    lax.fori_loop(0, 2 * N, wait_final, 0)
    got_all = f_in[0].astype(F32)
    for m in range(1, 2 * N):
        got_all = got_all + f_in[m].astype(F32)
    dnormed = got_all[:ROWS]
    x = pad_s[...]
    grad = gain_row * dnormed * my_scale - x * (my_scale**3 * my_rowdot / (SF * 4 * N))
    gh_out[...] = grad[:, :SF]
    gg_out[...] = (got_all[ROWS:ROWS + 1] + got_all[ROWS + 1:ROWS + 2])[:, :SF]

    for copy in sent:
        copy.wait_send()

    def finish(m, _):
        @pl.when(away(m))
        def _():
            piece_send(m).wait_send()

        @pl.when(is_other(m))
        def _():
            final_send(m).wait_send()

        return 0

    lax.fori_loop(0, 2 * N, finish, 0)


def on_device(teacher_hidden, teacher_head, student_hidden, student_gain, student_head, token_mask):
    def shape(*dims):
        return jax.ShapeDtypeStruct(dims, F32)

    vmem = pl.BlockSpec(memory_space=pltpu.VMEM)
    anywhere = pl.BlockSpec(memory_space=pl.ANY)

    def half(*dims):
        return pltpu.VMEM(dims, BF16)

    def full(*dims):
        return pltpu.VMEM(dims, F32)

    dma = pltpu.SemaphoreType.DMA
    kl, loss, gh, gg = pl.pallas_call(
        body,
        out_shape=(shape(1, TOK), shape(1, 1), shape(ROWS, SF), shape(1, SF)),
        in_specs=[vmem, vmem, vmem, vmem, anywhere, anywhere],
        out_specs=(vmem, vmem, vmem, vmem),
        scratch_shapes=[
            half(4608, VOC), half(2304, VOC),
            half(4, VOC, 1152), half(2, VOC, 1152), half(16, TF, VOC),
            full(2304, 128), full(ROWS, 256), full(ROWS, 128),
            half(2 * ROWS, 128), half(16, 2 * ROWS, 128),
            half(32, TF, TOK), half(32, SP, TOK), half(16, TF, TOK),
            full(VOC, TOK), full(VOC, TOK), full(VOC, TOK), full(VOC, TOK),
            full(VOC, TOK), full(VOC, TOK), full(VOC, TOK), half(VOC, TOK),
            full(8, TOK), full(8, TOK), full(N, 8, TOK), full(N, 8, TOK), full(4, 8, TOK),
            full(TOK, 128),
            full(8, TF, TOK), half(8, TF, TOK), half(8, TF, TOK),
            half(8, TF, TOK), half(8, TF, TOK),
            half(SP, TOK), half(SP, TOK),
            half(16, 32, 128), half(16, 32, 128),
            dma((2,)), dma((16,)), dma((16,)), dma((2,)), dma((2,)),
            dma((32,)), dma((32,)), dma((32,)), dma((32,)),
            dma((1,)), dma((1,)), dma((8,)), dma((8,)), dma((8,)), dma((8,)), dma((3,)), dma((3,)),
            dma((8,)), dma((8,)), dma((8,)), dma((8,)), dma((1,)), dma((1,)), dma((16,)), dma((16,)),
        ],
        compiler_params=pltpu.CompilerParams(
            collective_id=0, has_side_effects=True, vmem_limit_bytes=56 * 1024 * 1024
        ),
        name="distill",
    )(
        teacher_hidden, student_hidden, student_gain.reshape(18, 128), token_mask.reshape(1, TOK),
        teacher_head, student_head,
    )
    return kl.reshape(TOK), loss.reshape(()), gh, gg.reshape(SF)


def solution(mesh):
    placed = (
        P("dp", "vocab"),
        P(None, ("dp", "vocab")),
        P("dp", "vocab"),
        P(),
        P(None, ("dp", "vocab")),
        P(),
    )
    return jax.shard_map(
        on_device,
        mesh=mesh,
        in_specs=placed,
        out_specs=(P(), P(), P("dp", "vocab"), P("vocab")),
        check_vma=False,
    )
```

time: 752 us -> 108 us (0.14)
  the two profiles are of different devices: /device:TPU:4 before, /device:TPU:8 now
where the time goes in v1:
time: 108 us
  Pallas kernels  100 us (93%)
  local copies, waits for them, and re-layouts  3.73 us (3%)
  between operations  2.41 us (2%)
  other arithmetic  1.27 us (1%)
    pallas_call x1, Pallas kernels, on_device(): pl.pallas_call(body, out_shape=(shape(1, TOK), shape(1, 1), shape(ROWS, S...  100 us
    unnamed x2, local copies, waits for them, and re-layouts  2.48 us

profile of v1, /device:TPU:8, one launch (start us, length us, event | category | flops | bytes accessed | tf_op | source)
XLA Modules:
  0.0 107.7 jit_solution(4771469633525365085)
XLA Ops:
  0.6 1.2 %reshape.24.mask = s32[1,384]{1,0:T(1,128)} reshape(s32[384]{0:T(512)} %param.11) | data formatting | bytes 3072 | tf_op jit(solution)/shard_map/reshape | solution.py:546
  1.9 100.3 %distill.1 = (f32[1,384]{1,0:T(1,128)}, f32[1,1]{1,0:T(1,128)}, f32[24,72]{1,0:T(8,128)}, f32[1,72]{1,0:T(1,128)}) custom-call(bf16[24,144]{1,0:T(8,128)(2,1)} %th.1, bf16[24,72]{1,0:T(8,128)(2,1)} %sh.1, f32[18,128]{1,0:T(8,128)} %bitcast.3, s32[1,384]{1,0:T(1,128)} %reshape.24.mask, bf16[4608,256]{1,0:T(8,128)(2,1)} %wt_hbm.1, bf16[2304,256]{1,0:T(8,128)(2,1)} %ws_hbm.1), custom_call_target="tpu_custom_call" | custom-call | tf_op jit(solution)/shard_map/distill/pallas_call | solution.py:517
  102.2 1.3 %reduce = f32[384]{0:T(512)} reduce(f32[1,384]{1,0:T(1,128)} %get-tuple-element.8, f32[]{:T(128)} %constant.4), dimensions={0}, to_apply=%get-tuple-element.8.reduce_sub_computation | reduce | bytes 3076 | tf_op jit(solution)/shard_map/distill/pallas_call | solution.py:517
  104.1 1.3 %copy.14 = f32[24,72]{1,0:T(8,128)} copy(f32[24,72]{1,0:T(8,128)} %get-tuple-element.18) | data formatting | bytes 13824
  105.4 1.2 %copy.15 = f32[72]{0:T(128)} copy(f32[72]{0:T(128)} %bitcast.4) | data formatting | bytes 576

commit v2 on v1

v2 whole, which is shorter than its diff:
```python
import jax
import jax.numpy as jnp
from jax import lax
from jax.experimental import pallas as pl
from jax.experimental.pallas import tpu as pltpu
from jax.sharding import PartitionSpec as P

F32, BF16 = jnp.float32, jnp.bfloat16
MESH = pl.DeviceIdType.MESH
N = 8
TOK, ROWS = 384, 24
TF, SF = 144, 72
SP = 80
VOC = 256
STOP = 99


def body(
    th, sh, gain, mask, wt_hbm, ws_hbm,
    kl_out, loss_out, gh_out, gg_out,
    wt, ws, wtt, wst0, wst1, wsr, gb, grow, perm, pad_t, pad_s, piece, got, xt, xs, ns0, ns1, sq, scol,
    ls, lt, pu, ep, qq, ql, et, dpu, s_own, s_sib, s_z, s_y, s_x, d_own, d_sib, d_z, d_y, d_x, cols, xturn, held,
    g_own, g_out, g_in, r_out, r_in, e_out, e_in, f_out, f_in,
    w_sem, p_send, p_recv, h_send, h_recv, ring_send, ring_recv, sib_send, sib_recv,
    a_send, a_recv, z_send, z_recv, y_send, y_recv, x_send, x_recv,
    gs_send, gs_recv, rr_send, rr_recv, e_send, e_recv, f_send, f_recv,
):
    d, v = lax.axis_index("dp"), lax.axis_index("vocab")
    xl, y = d // N, d % N
    s, z, xh = v % 2, (v // 2) % N, v // (2 * N)
    first = s == 0
    p = jnp.where(first, z, y)
    q = jnp.where(first, y, z)

    def dev(xl, y, xh, z, s):
        return (xl * N + y, (xh * N + z) * 2 + s)

    def ring(place):
        return dev(xl, jnp.where(first, y, place), xh, jnp.where(first, place, z), s)

    def group(m):
        j = m % N
        return dev(m // N, jnp.where(first, j, y), xh, jnp.where(first, z, j), s)

    def owner(m):
        return dev(m // N, m % N, xh, p, s)

    slot = xl * N + q
    self_in = jnp.logical_or(first, y == z)
    right, left = ring((p + 1) % N), ring((p + N - 1) % N)
    sibling = dev(xl, y, xh, z, 1 - s)
    across = dev(1 - xl, y, 1 - xh, z, s)

    def remote(src, dst, send, recv, to):
        return pltpu.make_async_remote_copy(
            src_ref=src, dst_ref=dst, send_sem=send, recv_sem=recv, device_id=to, device_id_type=MESH
        )

    wt_copy = pltpu.make_async_copy(wt_hbm, wt, w_sem.at[0])
    ws_copy = pltpu.make_async_copy(ws_hbm, ws, w_sem.at[1])
    wt_copy.start()
    ws_copy.start()

    barrier = pltpu.get_barrier_semaphore()

    def tell(to):
        pl.semaphore_signal(barrier, inc=1, device_id=to, device_id_type=MESH)

    def greet(i, _):
        tell(group((slot + i) % (2 * N)))
        return 0

    for to in (right, left, sibling, across):
        tell(to)
    lax.fori_loop(1, 2 * N, greet, 0)

    pad_t[...] = jnp.zeros_like(pad_t)
    pad_s[...] = jnp.zeros_like(pad_s)
    pad_t[:, :TF] = th[...].astype(F32)
    pad_s[:, :SF] = sh[...].astype(F32)
    lane = lax.broadcasted_iota(jnp.int32, (ROWS, 128), 1)
    low = jnp.where(lane < TF - 128, pad_t[:, 128:256], pltpu.roll(pad_s[...], TF - 128, 1))
    piece[...] = jnp.concatenate([pad_t[:, :128], low], axis=0).astype(BF16)

    got[slot] = piece[...]
    pl.semaphore_wait(barrier, 2 * N - 1 + 4)

    def piece_send(m):
        return remote(piece, got.at[slot], p_send.at[m], p_recv.at[slot], group(m))

    def send_pieces(i, _):
        piece_send((slot + i) % (2 * N)).start()
        return 0

    lax.fori_loop(1, 2 * N, send_pieces, 0)

    for i in range(18):
        gb[i * 128:(i + 1) * 128, :] = jnp.broadcast_to(gain[i:i + 1, :], (128, 128)).T
    ws_copy.wait()

    def reorder(c, _):
        one = ws[pl.ds(pl.multiple_of(c * TF, 16), TF), :].astype(F32)
        two = ws[pl.ds(pl.multiple_of((N + c) * TF, 16), TF), :].astype(F32)
        wsr[c] = jnp.concatenate([one[:SF], two[:SF]], axis=0).astype(BF16)
        wsr[N + c] = jnp.concatenate([one[SF:], two[SF:]], axis=0).astype(BF16)
        return 0

    lax.fori_loop(0, N, reorder, 0)

    for j in range(9):
        block = wsr[0:N].reshape(N * TF, VOC)[j * 128:(j + 1) * 128]
        wst0[:, j * 128:(j + 1) * 128] = block.T
    for h in (0, 1):
        rows = [wsr[N + c].astype(F32)[h * SF:(h + 1) * SF] for c in range(N)]
        rows = jnp.concatenate(rows + [jnp.zeros((64, VOC), F32)], axis=0).astype(BF16)
        gains = [gb[((h * N + c) * 2 + 1) * SF:((h * N + c) * 2 + 2) * SF, :] for c in range(N)]
        gains = jnp.concatenate(gains + [jnp.zeros((64, 128), F32)], axis=0)
        for j in range(5):
            at = slice(j * 128, (j + 1) * 128)
            wst1[h, :, at] = rows[at].T
            grow[h, :, at] = gains[at].T[:8]

    at = lax.broadcasted_iota(jnp.int32, (TOK, TOK), 1)
    group_of = (at * 2731) >> 16
    token = ((group_of & 1) * N + (group_of >> 1)) * ROWS + (at - group_of * ROWS)
    perm[...] = (token == lax.broadcasted_iota(jnp.int32, (TOK, TOK), 0)).astype(F32).astype(BF16)

    def turn_teacher(i):
        core, h = i // 2, i % 2
        base = [((h * N + c) * 2 + core) * TF for c in range(N)]
        if core == 0:
            rows = jnp.concatenate([wt[b:b + TF, :] for b in base], axis=0)
            blocks = [rows[j * 128:(j + 1) * 128] for j in range(9)]
        else:
            blocks = [wt[b:b + 128, :] for b in base]
            blocks.append(jnp.concatenate([wt[b + 128:b + TF, :] for b in base], axis=0))
        for j, block in enumerate(blocks):
            wtt[i, :, j * 128:(j + 1) * 128] = block.T

    def wait_pieces(i, _):
        m = (slot + i) % (2 * N)
        remote(piece, got.at[m], p_send.at[m], p_recv.at[m], sibling).wait_recv()
        return 0

    lax.fori_loop(1, 2 * N, wait_pieces, 0)

    mine = s * 2 * N + xh * N + p
    tail = TF - 128

    @pl.when(first)
    def _():
        pieces = [got[a * N + j].astype(F32) for j in range(N) for a in (0, 1)]
        upper = jnp.concatenate([t[:ROWS] for t in pieces], axis=0).T
        lower = jnp.concatenate([t[ROWS:] for t in pieces], axis=0).T
        for c in range(3):
            at = slice(c * 128, (c + 1) * 128)
            xt[mine, c * TF:(c + 1) * TF, :] = jnp.concatenate([upper[:, at], lower[:tail, at]], axis=0).astype(BF16)
            xs[mine, c * SP:(c + 1) * SP, :] = lower[tail:tail + SP, at].astype(BF16)

    @pl.when(jnp.logical_not(first))
    def _():
        lanes = lax.broadcasted_iota(jnp.int32, (2 * ROWS, 128), 1)
        blank = jnp.zeros((2 * ROWS, 128), F32)
        rest, student = blank, [blank] * 5
        for j in range(N):
            one, two = got[j].astype(F32), got[N + j].astype(F32)
            upper = jnp.concatenate([one[:ROWS], two[:ROWS]], axis=0)
            lower = jnp.concatenate([one[ROWS:], two[ROWS:]], axis=0)
            xt[mine, j * 48:(j + 1) * 48, :] = upper.astype(BF16)
            turned = pltpu.roll(lower, tail * j, 1) if j else lower
            rest = jnp.where(jnp.logical_and(lanes >= tail * j, lanes < tail * (j + 1)), turned, rest)
            a, b = SF * j // 128, SF * j % 128
            turned = pltpu.roll(lower, (b - tail) % 128, 1) if b != tail else lower
            student[a] = jnp.where(jnp.logical_and(lanes >= b, lanes < b + SF), turned, student[a])
            if b + SF > 128:
                student[a + 1] = jnp.where(lanes < b + SF - 128, turned, student[a + 1])
        xt[mine, 8 * 48:9 * 48, :] = rest.astype(BF16)
        for c in range(5):
            xs[mine, c * 48:(c + 1) * 48, :] = student[c].astype(BF16)

    def unit(core, place, other, teacher):
        half = 1 - xh if other else xh
        i = core * 2 * N + half * N + place
        return xt.at[i] if teacher else xs.at[i]

    sent = []

    def push(ref, send, recv, to):
        copy = remote(ref, ref, send, recv, to)
        copy.start()
        sent.append(copy)

    for kind in (0, 1):
        push(unit(s, p, 0, kind), h_send.at[kind], h_recv.at[kind], across)

    units = [(0, 0), (0, 1), (1, 0), (1, 1)]

    def to_ring(way, step, u, place):
        i = (way * 4 + step) * 4 + u
        push(unit(s, place, *units[u]), ring_send.at[i], ring_recv.at[i], (right, left)[way])

    def from_ring(way, step, u, place):
        i = (way * 4 + step) * 4 + u
        ref = unit(s, place, *units[u])
        remote(ref, ref, ring_send.at[i], ring_recv.at[i], sibling).wait_recv()

    def to_sibling(slot, u, place):
        i = slot * 4 + u
        push(unit(s, place, *units[u]), sib_send.at[i], sib_recv.at[i], sibling)

    def from_sibling(slot, u, place):
        i = slot * 4 + u
        ref = unit(1 - s, place, *units[u])
        remote(ref, ref, sib_send.at[i], sib_recv.at[i], sibling).wait_recv()

    def behind(place, way, step):
        return (place + (N - step if way == 0 else step)) % N

    def from_across(kind):
        ref = unit(s, p, 1, kind)
        remote(ref, ref, h_send.at[kind], h_recv.at[kind], sibling).wait_recv()

    def start_ring(u):
        to_ring(0, 0, u, p)
        to_ring(1, 0, u, p)
        to_sibling(0, u, p)

    def go_round(step, other):
        for kind in (0, 1):
            u = units.index((other, kind))
            for way in (0, 1):
                place = behind(p, way, step)
                from_ring(way, step - 1, u, place)
                if step < 3 or other == way:
                    to_ring(way, step, u, place)
                to_sibling(way * 3 + step, u, place)

    start_ring(0)
    start_ring(1)
    wt_copy.wait()
    turn_teacher(0)
    go_round(1, 0)
    from_across(0)
    start_ring(2)
    from_across(1)
    start_ring(3)
    turn_teacher(1)
    go_round(2, 0)
    go_round(1, 1)
    turn_teacher(2)
    go_round(3, 0)
    go_round(2, 1)
    turn_teacher(3)
    go_round(3, 1)

    far, sib_far = behind(p, 0, 4), behind(q, 0, 4)

    def last(kind):
        for way in (0, 1):
            u = units.index((way, kind))
            from_ring(way, 3, u, far)
            to_sibling(7, u, far)

    def all_from_sibling(kind):
        for other in (0, 1):
            u = units.index((other, kind))
            from_sibling(0, u, q)
            for step in (1, 2, 3):
                for way in (0, 1):
                    from_sibling(way * 3 + step, u, behind(q, way, step))
            from_sibling(7, u, sib_far)

    last(0)
    all_from_sibling(0)

    def squares(i, total):
        parts = []
        for c in range(3):
            x = xs[i, c * SP:(c + 1) * SP, :].astype(F32)
            part = x[0:8] * x[0:8]
            for j in range(1, SF // 8):
                part = part + x[j * 8:(j + 1) * 8] * x[j * 8:(j + 1) * 8]
            parts.append(part)
        return total + jnp.concatenate(parts, axis=1)

    def squares_rows(j, _):
        part = jnp.zeros((48, 128), F32)
        for h in (0, 1):
            for c in range(5):
                x = xs[2 * N + h * N + j, c * 48:(c + 1) * 48, :].astype(F32)
                part = part + x * x
        sq[pl.ds(pl.multiple_of(j * 48, 48), 48), :] = part
        return 0

    total = lax.fori_loop(0, 2 * N, squares, jnp.zeros((8, TOK), F32))
    lax.fori_loop(0, N, squares_rows, 0)
    total = jnp.sum(total, axis=0, keepdims=True) + jnp.sum(sq[...].T, axis=0, keepdims=True)
    scale = lax.rsqrt(total / (SF * 4 * N) + 1e-6)
    scol[...] = jnp.broadcast_to(scale, (128, TOK)).T

    def features_first(i):
        x = xs[i].astype(F32)
        return jnp.concatenate([x[c * SP:c * SP + SF] for c in range(3)], axis=1)

    def normalise(c, _):
        for half in (0, 1):
            at = pl.multiple_of((half * N + c) * 2 * SF, 8)
            g = gb[pl.ds(at, SF), :]
            n = (features_first(half * N + c) * scale) * jnp.concatenate([g, g, g], axis=1)
            if half == 0:
                head = n
        ns0[c] = jnp.concatenate([head, n], axis=0).astype(BF16)
        return 0

    def normalise_rows(j, _):
        at = pl.ds(pl.multiple_of(j * 48, 48), 48)
        sc = scol[at, :]
        for h in (0, 1):
            for c in range(5):
                x = xs[2 * N + h * N + j, c * 48:(c + 1) * 48, :].astype(F32)
                n = (x * sc) * grow[h, 0:1, c * 128:(c + 1) * 128]
                ns1[h, at, c * 128:(c + 1) * 128] = n.astype(BF16)
        return 0

    lax.fori_loop(0, N, normalise, 0)
    lax.fori_loop(0, N, normalise_rows, 0)

    def dot(a, b):
        return jnp.dot(a, b, preferred_element_type=F32)

    def dot_rows(a, b):
        return lax.dot_general(a, b, (((1,), (1,)), ((), ())), preferred_element_type=F32)

    ls[...] = dot(wst0[...], ns0[...].reshape(N * TF, TOK))
    ls[...] += dot_rows(wst1[0], ns1[0])
    ls[...] += dot_rows(wst1[1], ns1[1])

    step_rows = 32

    def fold(x):
        out = x[0:8]
        for j in range(1, step_rows // 8):
            out = out + x[j * 8:(j + 1) * 8]
        return out

    zero = jnp.zeros((8, TOK), F32)

    def student(i, carry):
        at = pl.ds(pl.multiple_of(i * step_rows, step_rows), step_rows)
        logit = ls[at, :]
        pupil = 30.0 * jnp.tanh(logit / 30.0)
        e = jnp.exp(pupil - 30.0)
        slope = 1.0 - (pupil / 30.0) ** 2
        pu[at, :], ep[at, :], qq[at, :] = pupil, e, slope
        sl = slope * logit
        ql[at, :] = sl
        return carry[0] + fold(e), carry[1] + fold(e * sl)

    zs8, u8 = lax.fori_loop(0, VOC // step_rows, student, (zero, zero))

    last(1)
    all_from_sibling(1)

    def tokens_last(h):
        cs = [xt[h * N:(h + 1) * N, c * TF:(c + 1) * TF, :].reshape(N * TF, 128) for c in range(3)]
        return jnp.concatenate(cs, axis=1)

    def tokens_first(h):
        at = 2 * N + h * N
        cs = [xt[at:at + N, c * 48:(c + 1) * 48, :].reshape(TOK, 128) for c in range(9)]
        return jnp.concatenate(cs, axis=1)

    lt[...] = dot(wtt[0], tokens_last(0))
    lt[...] += dot(wtt[1], tokens_last(1))
    lt[...] += dot_rows(wtt[2], tokens_first(0))
    lt[...] += dot_rows(wtt[3], tokens_first(1))

    def teacher(i, carry):
        at = pl.ds(pl.multiple_of(i * step_rows, step_rows), step_rows)
        teach = 30.0 * jnp.tanh(lt[at, :] / 30.0)
        e = jnp.exp(teach - 30.0)
        et[at, :] = e
        return (
            carry[0] + fold(e),
            carry[1] + fold(e * (teach - pu[at, :])),
            carry[2] + fold(e * ql[at, :]),
        )

    zt8, c8, v8 = lax.fori_loop(0, VOC // step_rows, teacher, (zero, zero, zero))
    fold8 = [jnp.sum(t, axis=0, keepdims=True) for t in (zt8, zs8, c8, u8, v8)]
    s_own[...] = jnp.concatenate(fold8[:3] + [jnp.zeros((1, TOK), F32)], axis=0)
    d_own[...] = jnp.concatenate(fold8[3:], axis=0)

    def core_start(own, sib, k):
        copy = remote(own, sib, a_send.at[k], a_recv.at[k], sibling)
        copy.start()
        sent.append(copy)
        return copy

    def line_start(buf, send, recv, k, here, who, value):
        buf[here] = value
        for j in range(1, N):
            i = k * N + j
            copy = remote(buf.at[here], buf.at[here], send.at[i], recv.at[i], who((here + j) % N))
            copy.start()
            sent.append(copy)

    def line_end(buf, send, recv, k, here):
        for j in range(1, N):
            i, at = k * N + j, (here + N - j) % N
            remote(buf.at[at], buf.at[at], send.at[i], recv.at[i], sibling).wait_recv()
        out = buf[0]
        for j in range(1, N):
            out = out + buf[j]
        return out

    others = ((1 - xl, xh), (xl, 1 - xh), (1 - xl, 1 - xh))

    def x_start(buf, k, value):
        here = xh * 2 + xl
        buf[here] = value
        for j, (a, b) in enumerate(others):
            i = k * 3 + j
            copy = remote(buf.at[here], buf.at[here], x_send.at[i], x_recv.at[i], dev(a, y, b, z, s))
            copy.start()
            sent.append(copy)

    def x_end(buf, k):
        for j, (a, b) in enumerate(others):
            i, at = k * 3 + j, b * 2 + a
            remote(buf.at[at], buf.at[at], x_send.at[i], x_recv.at[i], sibling).wait_recv()
        return buf[0] + buf[1] + buf[2] + buf[3]

    def along_z(t):
        return dev(xl, y, xh, t, s)

    def along_y(t):
        return dev(xl, t, xh, z, s)

    main = core_start(s_own, s_sib, 0)
    late = core_start(d_own, d_sib, 1)
    main.wait_recv()
    line_start(s_z, z_send, z_recv, 0, z, along_z, s_own[...] + s_sib[...])
    late.wait_recv()
    late_value = d_own[...] + d_sib[...]
    value = line_end(s_z, z_send, z_recv, 0, z)
    line_start(s_y, y_send, y_recv, 0, y, along_y, value)
    line_start(d_z, z_send, z_recv, 1, z, along_z, late_value)
    value = line_end(s_y, y_send, y_recv, 0, y)
    x_start(s_x, 0, value)
    late_value = line_end(d_z, z_send, z_recv, 1, z)
    line_start(d_y, y_send, y_recv, 1, y, along_y, late_value)
    value = x_end(s_x, 0)
    zt, zs, cross = (value[i:i + 1] for i in range(3))

    maskf = jnp.broadcast_to(mask[...].astype(F32).reshape(1, TOK), (16, TOK)).astype(BF16)
    maskf = dot(maskf, perm[...])[0:1]
    weight = maskf / jnp.maximum(jnp.sum(maskf, axis=1, keepdims=True), 1.0)
    token_kl = cross / zt - jnp.log(zt) + jnp.log(zs)
    over_s, over_t = weight / zs, weight / zt

    def gradient(i, _):
        at = pl.ds(pl.multiple_of(i * step_rows, step_rows), step_rows)
        dpu[at, :] = ((ep[at, :] * over_s - et[at, :] * over_t) * qq[at, :]).astype(BF16)
        return 0

    lax.fori_loop(0, VOC // step_rows, gradient, 0)

    offsets = (4, 3, -3, 2, -2, 1, -1, 0)
    w_all = dpu[...]

    def chunk(i):
        off = offsets[i]
        g_out[i] = dot(wsr[(1 - s) * N + (q + off + N) % N], w_all).astype(BF16)
        copy = remote(g_out.at[i], g_in.at[i], gs_send.at[i], gs_recv.at[i], sibling)
        copy.start()
        sent.append(copy)
        g_own[i] = dot(wsr[s * N + (p + off + N) % N], w_all)

    def own(i):
        remote(g_out.at[i], g_in.at[i], gs_send.at[i], gs_recv.at[i], sibling).wait_recv()
        g_own[i] = g_own[i] + g_in[i].astype(F32)

    parts = (0, SP), (SP, 2 * SF)

    def hop(way, step, part, i):
        at, (lo, hi) = way * 4 + step, parts[part]
        value = g_own[i, lo:hi, :]
        if step > 1 or (step == 1 and part == way):
            value = value + arrive(way, step - 1, part)
        r_out[at, lo:hi, :] = value.astype(BF16)
        copy = remote(
            r_out.at[at, lo:hi], r_in.at[at, lo:hi], rr_send.at[at * 2 + part], rr_recv.at[at * 2 + part],
            (right, left)[way],
        )
        copy.start()
        sent.append(copy)

    def arrive(way, step, part):
        at, (lo, hi) = way * 4 + step, parts[part]
        remote(
            r_out.at[at, lo:hi], r_in.at[at, lo:hi], rr_send.at[at * 2 + part], rr_recv.at[at * 2 + part], sibling
        ).wait_recv()
        return r_in[at, lo:hi, :].astype(F32)

    chunk(0)
    chunk(1)
    chunk(2)
    own(0)
    hop(0, 0, 0, 0)
    hop(1, 0, 1, 0)
    own(1)
    hop(0, 1, 1, 1)
    own(2)
    hop(1, 1, 0, 2)
    chunk(3)
    chunk(4)
    hop(0, 1, 0, 1)
    hop(1, 1, 1, 2)
    own(3)
    own(4)
    chunk(5)
    chunk(6)
    chunk(7)
    hop(0, 2, 1, 3)
    hop(1, 2, 0, 4)
    hop(0, 2, 0, 3)
    hop(1, 2, 1, 4)
    own(5)
    own(6)
    own(7)

    late_value = line_end(d_y, y_send, y_recv, 1, y)
    x_start(d_x, 1, late_value)
    loss_out[...] = jnp.sum(weight * token_kl, axis=1, keepdims=True)
    rest, split = token_kl, []
    for _ in range(3):
        split.append(rest.astype(BF16).astype(F32))
        rest = rest - split[-1]
    split = jnp.concatenate(split + [jnp.zeros((13, TOK), F32)], axis=0).astype(BF16)
    placed = dot_rows(split, perm[...])
    kl_out[...] = (placed[0:1] + placed[1:2]) + placed[2:3]

    @pl.when(first)
    def _():
        held[...] = features_first(xh * N + p) * scale

    @pl.when(jnp.logical_not(first))
    def _():
        for c in range(5):
            x = xs[pl.ds(2 * N + xh * N, N), c * 48:(c + 1) * 48, :].reshape(TOK, 128).astype(F32)
            xturn[c * 128:(c + 1) * 128, :] = x.T
        held[...] = xturn[pl.ds(pl.multiple_of(p * SF, 8), SF), :] * scale

    hop(0, 3, 1, 5)
    hop(1, 3, 0, 6)
    hop(0, 3, 0, 5)
    hop(1, 3, 1, 6)
    late_value = x_end(d_x, 1)
    rowdot = (late_value[0:1] * over_s - late_value[1:2] * over_t) / scale
    stacked = jnp.concatenate([scale, rowdot, jnp.zeros((126, TOK), F32)], axis=0)
    cols[...] = stacked.T
    for part in (0, 1):
        lo, hi = parts[part]
        g_own[0, lo:hi, :] = g_own[7, lo:hi, :] + arrive(0, 3, part) + arrive(1, 3, part)

    give = g_own[0, pl.ds(pl.multiple_of((1 - xh) * SF, 8), SF), :]
    e_out[...] = jnp.concatenate([give, jnp.zeros((SP - SF, TOK), F32)], axis=0).astype(BF16)
    copy = remote(e_out, e_in, e_send.at[0], e_recv.at[0], across)
    copy.start()
    sent.append(copy)
    keep = g_own[0, pl.ds(pl.multiple_of(xh * SF, 8), SF), :]
    x_held = held[...]
    gains = gb[pl.ds(pl.multiple_of(v * SF, 8), SF), :]
    filler = jnp.zeros((128 - SF, 128), F32)
    gain_row = jnp.concatenate([gains, filler], axis=0).T[:ROWS]
    mycols = cols[pl.ds(pl.multiple_of((y * 2 + xl) * ROWS, 8), ROWS), :]
    my_scale, my_rowdot = mycols[:, 0:1], mycols[:, 1:2]
    copy.wait_recv()
    keep = keep + e_in[...].astype(F32)[:SF]
    gain_grad = jnp.sum(keep * x_held, axis=1, keepdims=True)
    gain_grad = jnp.concatenate([jnp.broadcast_to(gain_grad, (SF, 128)), filler], axis=0).T[:8]
    rough = gain_grad.astype(BF16).astype(F32)
    row = lax.broadcasted_iota(jnp.int32, (8, 128), 0)
    gain_grad = jnp.where(row == 0, rough, gain_grad - rough)
    keep = jnp.concatenate([keep, jnp.zeros((128 - SF, TOK), F32)], axis=0).T
    for m in range(2 * N):
        at = ((m % N) * 2 + m // N) * ROWS
        f_out[m] = jnp.concatenate([keep[at:at + ROWS], gain_grad], axis=0).astype(BF16)

    def final_send(m):
        return remote(f_out.at[m], f_in.at[slot], f_send.at[m], f_recv.at[slot], owner(m))

    def is_other(m):
        who = owner(m)
        return jnp.logical_not(jnp.logical_and(who[0] == d, who[1] == v))

    def send_final(i, _):
        m = (d + 1 + i) % (2 * N)

        @pl.when(is_other(m))
        def _():
            final_send(m).start()

        return 0

    lax.fori_loop(0, 2 * N, send_final, 0)

    @pl.when(self_in)
    def _():
        f_in[slot] = f_out[d]

    def wait_final(m, _):
        @pl.when(jnp.logical_not(jnp.logical_and(self_in, m == slot)))
        def _():
            remote(f_out.at[m], f_in.at[m], f_send.at[m], f_recv.at[m], sibling).wait_recv()

        return 0

    lax.fori_loop(0, 2 * N, wait_final, 0)
    got_all = f_in[0].astype(F32)
    for m in range(1, 2 * N):
        got_all = got_all + f_in[m].astype(F32)
    dnormed = got_all[:ROWS]
    x = pad_s[...]
    grad = gain_row * dnormed * my_scale - x * (my_scale**3 * my_rowdot / (SF * 4 * N))
    gh_out[...] = grad[:, :SF]
    gg_out[...] = (got_all[ROWS:ROWS + 1] + got_all[ROWS + 1:ROWS + 2])[:, :SF]

    for copy in sent:
        copy.wait_send()

    def finish(m, _):
        @pl.when(m != slot)
        def _():
            piece_send(m).wait_send()

        @pl.when(is_other(m))
        def _():
            final_send(m).wait_send()

        return 0

    lax.fori_loop(0, 2 * N, finish, 0)


def outputs(kl, loss, gh, gg, kl_out, loss_out, gh_out, gg_out):
    kl_out[...] = kl[...].reshape(TOK)
    loss_out[...] = loss[...]
    gh_out[...] = gh[...]
    gg_out[...] = gg[...].reshape(SF)


def on_device(teacher_hidden, teacher_head, student_hidden, student_gain, student_head, token_mask):
    def shape(*dims):
        return jax.ShapeDtypeStruct(dims, F32)

    vmem = pl.BlockSpec(memory_space=pltpu.VMEM)
    anywhere = pl.BlockSpec(memory_space=pl.ANY)

    def half(*dims):
        return pltpu.VMEM(dims, BF16)

    def full(*dims):
        return pltpu.VMEM(dims, F32)

    dma = pltpu.SemaphoreType.DMA
    kl, loss, gh, gg = pl.pallas_call(
        body,
        out_shape=(shape(1, TOK), shape(1, 1), shape(ROWS, SF), shape(1, SF)),
        in_specs=[vmem, vmem, vmem, vmem, anywhere, anywhere],
        out_specs=(vmem, vmem, vmem, vmem),
        scratch_shapes=[
            half(4608, VOC), half(2304, VOC),
            half(4, VOC, 1152), half(VOC, 1152), half(2, VOC, 640), half(16, TF, VOC),
            full(2304, 128), full(2, 8, 640), half(TOK, TOK),
            full(ROWS, 256), full(ROWS, 128),
            half(2 * ROWS, 128), half(16, 2 * ROWS, 128),
            half(32, 3 * TF, 128), half(32, 3 * SP, 128),
            half(N, TF, TOK), half(2, TOK, 640), full(TOK, 128), full(TOK, 128),
            full(VOC, TOK), full(VOC, TOK), full(VOC, TOK), full(VOC, TOK),
            full(VOC, TOK), full(VOC, TOK), full(VOC, TOK), half(VOC, TOK),
            full(4, TOK), full(4, TOK), full(N, 4, TOK), full(N, 4, TOK), full(4, 4, TOK),
            full(2, TOK), full(2, TOK), full(N, 2, TOK), full(N, 2, TOK), full(4, 2, TOK),
            full(TOK, 128), full(640, TOK), full(SF, TOK),
            full(8, TF, TOK), half(8, TF, TOK), half(8, TF, TOK),
            half(8, TF, TOK), half(8, TF, TOK),
            half(SP, TOK), half(SP, TOK),
            half(16, 32, 128), half(16, 32, 128),
            dma((2,)), dma((16,)), dma((16,)), dma((2,)), dma((2,)),
            dma((32,)), dma((32,)), dma((32,)), dma((32,)),
            dma((2,)), dma((2,)), dma((16,)), dma((16,)), dma((16,)), dma((16,)), dma((6,)), dma((6,)),
            dma((8,)), dma((8,)), dma((16,)), dma((16,)), dma((1,)), dma((1,)), dma((16,)), dma((16,)),
        ],
        compiler_params=pltpu.CompilerParams(
            collective_id=0, has_side_effects=True, vmem_limit_bytes=56 * 1024 * 1024
        ),
        name="distill",
    )(
        teacher_hidden, student_hidden, student_gain.reshape(18, 128), token_mask,
        teacher_head, student_head,
    )
    kl, loss, gh, gg = pl.pallas_call(
        outputs,
        out_shape=(shape(TOK), shape(1, 1), shape(ROWS, SF), shape(SF)),
        in_specs=[vmem] * 4,
        out_specs=(vmem,) * 4,
        name="outputs",
    )(kl, loss, gh, gg)
    return kl, loss.reshape(()), gh, gg


def solution(mesh):
    placed = (
        P("dp", "vocab"),
        P(None, ("dp", "vocab")),
        P("dp", "vocab"),
        P(),
        P(None, ("dp", "vocab")),
        P(),
    )
    return jax.shard_map(
        on_device,
        mesh=mesh,
        in_specs=placed,
        out_specs=(P(), P(), P("dp", "vocab"), P("vocab")),
        check_vma=False,
    )
```

time: 108 us -> 92 us (0.85)
  Pallas kernels: 100 us -> 91.1 us
  local copies, waits for them, and re-layouts: 3.73 us -> 0 us
  between operations: 2.41 us -> 0.64 us
  other arithmetic: 1.27 us -> 0 us
    pallas_call x1, Pallas kernels: 100 us -> 89.2 us  [on_device(): pl.pallas_call(body, out_shape=(shape(1, TOK), shape(1, 1), shape(ROWS, S...]
    unnamed x2 -> x0, local copies, waits for them, and re-layouts: 2.48 us -> none
    pallas_call x0 -> x1, Pallas kernels: none -> 1.93 us  [on_device(): pl.pallas_call(outputs, out_shape=(shape(TOK), shape(1, 1), shape(ROWS, S...]
    pallas_call x1 -> x0, other arithmetic: 1.27 us -> none  [on_device(): pl.pallas_call(body, out_shape=(shape(1, TOK), shape(1, 1), shape(ROWS, S...]
    reshape x1 -> x0, local copies, waits for them, and re-layouts: 1.25 us -> none  [on_device(): token_mask.reshape(1, TOK)]
where the time goes in v2:
time: 92 us; the launch traced here: 91.8 us
  Pallas kernels  91.1 us (99%)
    pallas_call x1, Pallas kernels, on_device(): pl.pallas_call(body, out_shape=(shape(1, TOK), shape(1, 1), shape(ROWS, S...  89.2 us
    pallas_call x1, Pallas kernels, on_device(): pl.pallas_call(outputs, out_shape=(shape(TOK), shape(1, 1), shape(ROWS, S...  1.93 us

profile of v2, /device:TPU:8, one launch (start us, length us, event | category | flops | bytes accessed | tf_op | source)
XLA Modules:
  0.0 91.8 jit_solution(12908405290054750849)
XLA Ops:
  0.6 89.2 %distill.1 = (f32[1,384]{1,0:T(1,128)}, f32[1,1]{1,0:T(1,128)}, f32[24,72]{1,0:T(8,128)}, f32[1,72]{1,0:T(1,128)}) custom-call(bf16[24,144]{1,0:T(8,128)(2,1)} %th.1, bf16[24,72]{1,0:T(8,128)(2,1)} %sh.1, f32[18,128]{1,0:T(8,128)} %bitcast.2, s32[384]{0:T(512)} %mask.1, bf16[4608,256]{1,0:T(8,128)(2,1)} %wt_hbm.1, bf16[2304,256]{1,0:T(8,128)(2,1)} %ws_hbm.1), custom_call_target="tpu_custom_call" | custom-call | tf_op jit(solution)/shard_map/distill/pallas_call | solution.py:668
  89.8 1.9 %outputs.1 = (f32[384]{0:T(512)}, f32[1,1]{1,0:T(1,128)}, f32[24,72]{1,0:T(8,128)}, f32[72]{0:T(128)}) custom-call(f32[1,384]{1,0:T(1,128)} %get-tuple-element.12.kl, f32[1,1]{1,0:T(1,128)} %get-tuple-element.13.loss, f32[24,72]{1,0:T(8,128)} %get-tuple-element.14.gh, f32[1,72]{1,0:T(1,128)} %get-tuple-element.15.gg), custom_call_target="tpu_custom_call" | custom-call | tf_op jit(solution)/shard_map/outputs/pallas_call | solution.py:703

commit v3 on v2

v3 whole, which is shorter than its diff:
```python
import jax
import jax.numpy as jnp
from jax import lax
from jax.experimental import pallas as pl
from jax.experimental.pallas import tpu as pltpu
from jax.sharding import PartitionSpec as P

F32, BF16 = jnp.float32, jnp.bfloat16
MESH = pl.DeviceIdType.MESH
N = 8
TOK, ROWS = 384, 24
TF, SF = 144, 72
SP = 80
VOC = 256
STOP = 99


def body(
    th, sh, gain, mask, wt_hbm, ws_hbm,
    kl_out, loss_out, gh_out, gg_out,
    wt, ws, wtt, wst0, wst1, wsr, gb, grow, perm, pad_t, pad_s, piece, got, xt, xs, ns0, ns1, sq, scol,
    ls, lt, pu, ep, qq, ql, et, dpu, s_z, s_y, s_x, d_z, d_y, d_x, cols, xturn, held,
    g_own, g_out, g_in, r_out, r_in, e_out, e_in, f_out, f_in,
    w_sem, p_send, p_recv, ring_send, ring_recv, sib_send, sib_recv,
    z_send, z_recv, y_send, y_recv, x_send, x_recv,
    gs_send, gs_recv, rr_send, rr_recv, e_send, e_recv, f_send, f_recv,
):
    d, v = lax.axis_index("dp"), lax.axis_index("vocab")
    xl, y = d // N, d % N
    s, z, xh = v % 2, (v // 2) % N, v // (2 * N)
    first = s == 0
    p = jnp.where(first, z, y)
    q = jnp.where(first, y, z)

    def dev(xl, y, xh, z, s):
        return (xl * N + y, (xh * N + z) * 2 + s)

    def ring(place):
        return dev(xl, jnp.where(first, y, place), xh, jnp.where(first, place, z), s)

    def member(dh, da, dj):
        j = (q + dj) % N
        return dev(xl ^ da, jnp.where(first, j, y), xh ^ dh, jnp.where(first, z, j), s)

    def owner(m):
        return dev(m // N, m % N, xh, p, s)

    slot = xl * N + q
    far_first = (4, 3, 5, 2, 6, 1, 7)
    line_mates = [
        (dh, da, dj) for dh in (0, 1) for dj in far_first + (0,) for da in (1, 0) if dh or da or dj
    ]
    self_in = jnp.logical_or(first, y == z)
    right, left = ring((p + 1) % N), ring((p + N - 1) % N)
    sibling = dev(xl, y, xh, z, 1 - s)
    across = dev(1 - xl, y, 1 - xh, z, s)

    def remote(src, dst, send, recv, to):
        return pltpu.make_async_remote_copy(
            src_ref=src, dst_ref=dst, send_sem=send, recv_sem=recv, device_id=to, device_id_type=MESH
        )

    wt_copy = pltpu.make_async_copy(wt_hbm, wt, w_sem.at[0])
    ws_copy = pltpu.make_async_copy(ws_hbm, ws, w_sem.at[1])
    wt_copy.start()
    ws_copy.start()

    barrier = pltpu.get_barrier_semaphore()

    def tell(to):
        pl.semaphore_signal(barrier, inc=1, device_id=to, device_id_type=MESH)

    for mate in line_mates:
        tell(member(*mate))
    for to in (right, left, sibling):
        tell(to)

    pad_t[...] = jnp.zeros_like(pad_t)
    pad_s[...] = jnp.zeros_like(pad_s)
    pad_t[:, :TF] = th[...].astype(F32)
    pad_s[:, :SF] = sh[...].astype(F32)
    lane = lax.broadcasted_iota(jnp.int32, (ROWS, 128), 1)
    low = jnp.where(lane < TF - 128, pad_t[:, 128:256], pltpu.roll(pad_s[...], TF - 128, 1))
    piece[...] = jnp.concatenate([pad_t[:, :128], low], axis=0).astype(BF16)

    got[xh * 2 * N + slot] = piece[...]
    pl.semaphore_wait(barrier, len(line_mates) + 3)
    sent = []

    for i, mate in enumerate(line_mates):
        copy = remote(piece, got.at[xh * 2 * N + slot], p_send.at[i], p_recv.at[i], member(*mate))
        copy.start()
        sent.append(copy)

    def wait_pieces(half):
        for i, (dh, da, dj) in enumerate(line_mates):
            if dh == half:
                at = ((xh ^ dh) * 2 + (xl ^ da)) * N + (q + N - dj) % N
                remote(piece, got.at[at], p_send.at[i], p_recv.at[i], sibling).wait_recv()

    for i in range(18):
        gb[i * 128:(i + 1) * 128, :] = jnp.broadcast_to(gain[i:i + 1, :], (128, 128)).T
    ws_copy.wait()

    def reorder(c, _):
        one = ws[pl.ds(pl.multiple_of(c * TF, 16), TF), :].astype(F32)
        two = ws[pl.ds(pl.multiple_of((N + c) * TF, 16), TF), :].astype(F32)
        wsr[c] = jnp.concatenate([one[:SF], two[:SF]], axis=0).astype(BF16)
        wsr[N + c] = jnp.concatenate([one[SF:], two[SF:]], axis=0).astype(BF16)
        return 0

    lax.fori_loop(0, N, reorder, 0)

    for j in range(9):
        block = wsr[0:N].reshape(N * TF, VOC)[j * 128:(j + 1) * 128]
        wst0[:, j * 128:(j + 1) * 128] = block.T
    for h in (0, 1):
        rows = [wsr[N + c].astype(F32)[h * SF:(h + 1) * SF] for c in range(N)]
        rows = jnp.concatenate(rows + [jnp.zeros((64, VOC), F32)], axis=0).astype(BF16)
        gains = [gb[((h * N + c) * 2 + 1) * SF:((h * N + c) * 2 + 2) * SF, :] for c in range(N)]
        gains = jnp.concatenate(gains + [jnp.zeros((64, 128), F32)], axis=0)
        for j in range(5):
            at = slice(j * 128, (j + 1) * 128)
            wst1[h, :, at] = rows[at].T
            grow[h, :, at] = gains[at].T[:8]

    at = lax.broadcasted_iota(jnp.int32, (TOK, TOK), 1)
    group_of = (at * 2731) >> 16
    token = ((group_of & 1) * N + (group_of >> 1)) * ROWS + (at - group_of * ROWS)
    perm[...] = (token == lax.broadcasted_iota(jnp.int32, (TOK, TOK), 0)).astype(F32).astype(BF16)

    def turn_teacher(i):
        core, h = i // 2, i % 2
        base = [((h * N + c) * 2 + core) * TF for c in range(N)]
        if core == 0:
            rows = jnp.concatenate([wt[b:b + TF, :] for b in base], axis=0)
            blocks = [rows[j * 128:(j + 1) * 128] for j in range(9)]
        else:
            blocks = [wt[b:b + 128, :] for b in base]
            blocks.append(jnp.concatenate([wt[b + 128:b + TF, :] for b in base], axis=0))
        for j, block in enumerate(blocks):
            wtt[i, :, j * 128:(j + 1) * 128] = block.T

    tail = TF - 128

    def assemble(half):
        base, mine = half * 2 * N, s * 2 * N + half * N + p

        @pl.when(first)
        def _():
            pieces = [got[base + a * N + j].astype(F32) for j in range(N) for a in (0, 1)]
            upper = jnp.concatenate([t[:ROWS] for t in pieces], axis=0).T
            lower = jnp.concatenate([t[ROWS:] for t in pieces], axis=0).T
            for c in range(3):
                at = slice(c * 128, (c + 1) * 128)
                xt[mine, c * TF:(c + 1) * TF, :] = jnp.concatenate([upper[:, at], lower[:tail, at]], axis=0).astype(BF16)
                xs[mine, c * SP:(c + 1) * SP, :] = lower[tail:tail + SP, at].astype(BF16)

        @pl.when(jnp.logical_not(first))
        def _():
            lanes = lax.broadcasted_iota(jnp.int32, (2 * ROWS, 128), 1)
            blank = jnp.zeros((2 * ROWS, 128), F32)
            rest, student = blank, [blank] * 5
            for j in range(N):
                one, two = got[base + j].astype(F32), got[base + N + j].astype(F32)
                upper = jnp.concatenate([one[:ROWS], two[:ROWS]], axis=0)
                lower = jnp.concatenate([one[ROWS:], two[ROWS:]], axis=0)
                xt[mine, j * 48:(j + 1) * 48, :] = upper.astype(BF16)
                turned = pltpu.roll(lower, tail * j, 1) if j else lower
                rest = jnp.where(jnp.logical_and(lanes >= tail * j, lanes < tail * (j + 1)), turned, rest)
                a, b = SF * j // 128, SF * j % 128
                turned = pltpu.roll(lower, (b - tail) % 128, 1) if b != tail else lower
                student[a] = jnp.where(jnp.logical_and(lanes >= b, lanes < b + SF), turned, student[a])
                if b + SF > 128:
                    student[a + 1] = jnp.where(lanes < b + SF - 128, turned, student[a + 1])
            xt[mine, 8 * 48:9 * 48, :] = rest.astype(BF16)
            for c in range(5):
                xs[mine, c * 48:(c + 1) * 48, :] = student[c].astype(BF16)

    def unit(core, place, other, part):
        i = core * 2 * N + (1 - xh if other else xh) * N + place
        if part == 0:
            return xs.at[i]
        return xt.at[i] if part == 4 else xt.at[i, (part - 1) * TF:part * TF]

    def push(ref, send, recv, to):
        copy = remote(ref, ref, send, recv, to)
        copy.start()
        sent.append(copy)

    def to_ring(way, step, other, part, place):
        i = (way * 4 + step) * 8 + other * 4 + part
        push(unit(s, place, other, part), ring_send.at[i], ring_recv.at[i], (right, left)[way])

    def from_ring(way, step, other, part, place):
        i = (way * 4 + step) * 8 + other * 4 + part
        ref = unit(s, place, other, part)
        remote(ref, ref, ring_send.at[i], ring_recv.at[i], sibling).wait_recv()

    def to_sibling(slot, other, part, place):
        if part in (0, 3):
            i = slot * 4 + other * 2 + part // 3
            push(unit(s, place, other, part and 4), sib_send.at[i], sib_recv.at[i], sibling)

    def from_sibling(slot, other, kind, place):
        i = slot * 4 + other * 2 + kind
        ref = unit(1 - s, place, other, kind * 4)
        remote(ref, ref, sib_send.at[i], sib_recv.at[i], sibling).wait_recv()

    def behind(place, way, step):
        return (place + (N - step if way == 0 else step)) % N

    def start_ring(other):
        for part in range(4):
            to_ring(0, 0, other, part, p)
            to_ring(1, 0, other, part, p)
            to_sibling(0, other, part, p)

    def go_round(step, other):
        for part in range(4):
            for way in (0, 1):
                place = behind(p, way, step)
                from_ring(way, step - 1, other, part, place)
                if step < 3 or other == way:
                    to_ring(way, step, other, part, place)
                to_sibling(way * 3 + step, other, part, place)

    wait_pieces(0)
    assemble(xh)
    start_ring(0)
    wait_pieces(1)
    assemble(1 - xh)
    start_ring(1)
    wt_copy.wait()
    turn_teacher(0)
    go_round(1, 0)
    go_round(1, 1)
    turn_teacher(1)
    go_round(2, 0)
    go_round(2, 1)
    turn_teacher(2)
    go_round(3, 0)
    go_round(3, 1)
    turn_teacher(3)

    far, sib_far = behind(p, 0, 4), behind(q, 0, 4)

    def last(parts):
        for part in parts:
            for way in (0, 1):
                from_ring(way, 3, way, part, far)
                to_sibling(7, way, part, far)

    def all_from_sibling(kind):
        for other in (0, 1):
            from_sibling(0, other, kind, q)
            for step in (1, 2, 3):
                for way in (0, 1):
                    from_sibling(way * 3 + step, other, kind, behind(q, way, step))
            from_sibling(7, other, kind, sib_far)

    def dot(a, b):
        return jnp.dot(a, b, preferred_element_type=F32)

    def dot_rows(a, b):
        return lax.dot_general(a, b, (((1,), (1,)), ((), ())), preferred_element_type=F32)

    def tokens_last(h):
        cs = [xt[h * N:(h + 1) * N, c * TF:(c + 1) * TF, :].reshape(N * TF, 128) for c in range(3)]
        return jnp.concatenate(cs, axis=1)

    def tokens_first(h):
        at = 2 * N + h * N
        cs = [xt[at:at + N, c * 48:(c + 1) * 48, :].reshape(TOK, 128) for c in range(9)]
        return jnp.concatenate(cs, axis=1)

    def teacher_dots(core):
        for h in (0, 1):
            lt[...] += dot_rows(wtt[2 + h], tokens_first(h)) if core else dot(wtt[h], tokens_last(h))

    last((0, 1, 2, 3))
    lt[...] = jnp.zeros_like(lt)

    @pl.when(first)
    def _():
        teacher_dots(0)

    @pl.when(jnp.logical_not(first))
    def _():
        teacher_dots(1)

    all_from_sibling(0)

    def squares(i, total):
        parts = []
        for c in range(3):
            x = xs[i, c * SP:(c + 1) * SP, :].astype(F32)
            part = x[0:8] * x[0:8]
            for j in range(1, SF // 8):
                part = part + x[j * 8:(j + 1) * 8] * x[j * 8:(j + 1) * 8]
            parts.append(part)
        return total + jnp.concatenate(parts, axis=1)

    def squares_rows(j, _):
        part = jnp.zeros((48, 128), F32)
        for h in (0, 1):
            for c in range(5):
                x = xs[2 * N + h * N + j, c * 48:(c + 1) * 48, :].astype(F32)
                part = part + x * x
        sq[pl.ds(pl.multiple_of(j * 48, 48), 48), :] = part
        return 0

    total = lax.fori_loop(0, 2 * N, squares, jnp.zeros((8, TOK), F32))
    lax.fori_loop(0, N, squares_rows, 0)
    total = jnp.sum(total, axis=0, keepdims=True) + jnp.sum(sq[...].T, axis=0, keepdims=True)
    scale = lax.rsqrt(total / (SF * 4 * N) + 1e-6)
    scol[...] = jnp.broadcast_to(scale, (128, TOK)).T

    def features_first(i):
        x = xs[i].astype(F32)
        return jnp.concatenate([x[c * SP:c * SP + SF] for c in range(3)], axis=1)

    def normalise(c, _):
        for half in (0, 1):
            at = pl.multiple_of((half * N + c) * 2 * SF, 8)
            g = gb[pl.ds(at, SF), :]
            n = (features_first(half * N + c) * scale) * jnp.concatenate([g, g, g], axis=1)
            if half == 0:
                head = n
        ns0[c] = jnp.concatenate([head, n], axis=0).astype(BF16)
        return 0

    def normalise_rows(j, _):
        at = pl.ds(pl.multiple_of(j * 48, 48), 48)
        sc = scol[at, :]
        for h in (0, 1):
            for c in range(5):
                x = xs[2 * N + h * N + j, c * 48:(c + 1) * 48, :].astype(F32)
                n = (x * sc) * grow[h, 0:1, c * 128:(c + 1) * 128]
                ns1[h, at, c * 128:(c + 1) * 128] = n.astype(BF16)
        return 0

    lax.fori_loop(0, N, normalise, 0)
    lax.fori_loop(0, N, normalise_rows, 0)

    ls[...] = dot(wst0[...], ns0[...].reshape(N * TF, TOK))
    ls[...] += dot_rows(wst1[0], ns1[0])
    ls[...] += dot_rows(wst1[1], ns1[1])

    step_rows = 32

    def fold(x):
        out = x[0:8]
        for j in range(1, step_rows // 8):
            out = out + x[j * 8:(j + 1) * 8]
        return out

    zero = jnp.zeros((8, TOK), F32)

    def student(i, carry):
        at = pl.ds(pl.multiple_of(i * step_rows, step_rows), step_rows)
        logit = ls[at, :]
        pupil = 30.0 * jnp.tanh(logit / 30.0)
        e = jnp.exp(pupil - 30.0)
        slope = 1.0 - (pupil / 30.0) ** 2
        pu[at, :], ep[at, :], qq[at, :] = pupil, e, slope
        sl = slope * logit
        ql[at, :] = sl
        return carry[0] + fold(e), carry[1] + fold(e * sl)

    zs8, u8 = lax.fori_loop(0, VOC // step_rows, student, (zero, zero))

    all_from_sibling(1)

    @pl.when(first)
    def _():
        teacher_dots(1)

    @pl.when(jnp.logical_not(first))
    def _():
        teacher_dots(0)


    def teacher(i, carry):
        at = pl.ds(pl.multiple_of(i * step_rows, step_rows), step_rows)
        teach = 30.0 * jnp.tanh(lt[at, :] / 30.0)
        e = jnp.exp(teach - 30.0)
        et[at, :] = e
        return (
            carry[0] + fold(e),
            carry[1] + fold(e * (teach - pu[at, :])),
            carry[2] + fold(e * ql[at, :]),
        )

    zt8, c8, v8 = lax.fori_loop(0, VOC // step_rows, teacher, (zero, zero, zero))
    fold8 = [jnp.sum(t, axis=0, keepdims=True) for t in (zt8, zs8, c8, u8, v8)]
    main_sums = jnp.concatenate(fold8[:2], axis=0)
    late_sums = jnp.concatenate(fold8[2:] + [jnp.zeros((1, TOK), F32)], axis=0)

    def line_start(buf, send, recv, k, here, who, value):
        buf[here] = value
        for j in far_first:
            i = k * N + j
            copy = remote(buf.at[here], buf.at[here], send.at[i], recv.at[i], who((here + j) % N))
            copy.start()
            sent.append(copy)

    def line_end(buf, send, recv, k, here):
        for j in range(1, N):
            i, at = k * N + j, (here + N - j) % N
            remote(buf.at[at], buf.at[at], send.at[i], recv.at[i], sibling).wait_recv()
        out = buf[0]
        for j in range(1, N):
            out = out + buf[j]
        return out

    others = [(dh, da, dc) for dh in (1, 0) for da in (1, 0) for dc in (0, 1) if dh or da or dc]

    def x_start(buf, k, value):
        here = (xh * 2 + xl) * 2 + s
        buf[here] = value
        for j, (dh, da, dc) in enumerate(others):
            i = k * 7 + j
            copy = remote(
                buf.at[here], buf.at[here], x_send.at[i], x_recv.at[i], dev(xl ^ da, y, xh ^ dh, z, s ^ dc)
            )
            copy.start()
            sent.append(copy)

    def x_end(buf, k):
        for j, (dh, da, dc) in enumerate(others):
            i, at = k * 7 + j, ((xh ^ dh) * 2 + (xl ^ da)) * 2 + (s ^ dc)
            remote(buf.at[at], buf.at[at], x_send.at[i], x_recv.at[i], sibling).wait_recv()
        out = buf[0]
        for j in range(1, 8):
            out = out + buf[j]
        return out

    def along_z(t):
        return dev(xl, y, xh, t, s)

    def along_y(t):
        return dev(xl, t, xh, z, s)

    line_start(s_z, z_send, z_recv, 0, z, along_z, main_sums)
    value = line_end(s_z, z_send, z_recv, 0, z)
    line_start(s_y, y_send, y_recv, 0, y, along_y, value)
    line_start(d_z, z_send, z_recv, 1, z, along_z, late_sums)
    value = line_end(s_y, y_send, y_recv, 0, y)
    x_start(s_x, 0, value)
    late_value = line_end(d_z, z_send, z_recv, 1, z)
    line_start(d_y, y_send, y_recv, 1, y, along_y, late_value)
    value = x_end(s_x, 0)
    zt, zs = value[0:1], value[1:2]

    maskf = jnp.broadcast_to(mask[...].astype(F32).reshape(1, TOK), (16, TOK)).astype(BF16)
    maskf = dot(maskf, perm[...])[0:1]
    weight = maskf / jnp.maximum(jnp.sum(maskf, axis=1, keepdims=True), 1.0)
    over_s, over_t = weight / zs, weight / zt

    def gradient(i, _):
        at = pl.ds(pl.multiple_of(i * step_rows, step_rows), step_rows)
        dpu[at, :] = ((ep[at, :] * over_s - et[at, :] * over_t) * qq[at, :]).astype(BF16)
        return 0

    lax.fori_loop(0, VOC // step_rows, gradient, 0)

    offsets = (4, 3, -3, 2, -2, 1, -1, 0)
    w_all = dpu[...]

    def chunk(i):
        off = offsets[i]
        g_out[i] = dot(wsr[(1 - s) * N + (q + off + N) % N], w_all).astype(BF16)
        copy = remote(g_out.at[i], g_in.at[i], gs_send.at[i], gs_recv.at[i], sibling)
        copy.start()
        sent.append(copy)
        g_own[i] = dot(wsr[s * N + (p + off + N) % N], w_all)

    def own(i):
        remote(g_out.at[i], g_in.at[i], gs_send.at[i], gs_recv.at[i], sibling).wait_recv()
        g_own[i] = g_own[i] + g_in[i].astype(F32)

    parts = (0, SP), (SP, 2 * SF)
    right2, left2 = ring((p + 2) % N), ring((p + N - 2) % N)

    def give(way, dist, part, i):
        at, (lo, hi) = way * 4 + dist - 1, parts[part]
        value = g_own[i, lo:hi, :]
        if dist == 2:
            value = value + take(way, 3, part)
            if part == way:
                value = value + take(way, 4, part)
        r_out[at, lo:hi, :] = value.astype(BF16)
        to = ((right, left), (right2, left2))[dist in (2, 4)][way]
        copy = remote(
            r_out.at[at, lo:hi], r_in.at[at, lo:hi], rr_send.at[at * 2 + part], rr_recv.at[at * 2 + part], to
        )
        copy.start()
        sent.append(copy)

    def take(way, dist, part):
        at, (lo, hi) = way * 4 + dist - 1, parts[part]
        remote(
            r_out.at[at, lo:hi], r_in.at[at, lo:hi], rr_send.at[at * 2 + part], rr_recv.at[at * 2 + part], sibling
        ).wait_recv()
        return r_in[at, lo:hi, :].astype(F32)

    chunk(0)
    chunk(1)
    chunk(2)
    own(0)
    give(0, 4, 0, 0)
    give(1, 4, 1, 0)
    own(1)
    give(0, 3, 1, 1)
    own(2)
    give(1, 3, 0, 2)
    give(0, 3, 0, 1)
    give(1, 3, 1, 2)
    for i in range(3, 8):
        chunk(i)
    own(5)
    own(6)
    for part in (0, 1):
        give(0, 1, part, 5)
        give(1, 1, part, 6)
    own(3)
    own(4)
    own(7)

    late_value = line_end(d_y, y_send, y_recv, 1, y)
    x_start(d_x, 1, late_value)
    @pl.when(first)
    def _():
        held[...] = features_first(xh * N + p) * scale

    @pl.when(jnp.logical_not(first))
    def _():
        for c in range(5):
            x = xs[pl.ds(2 * N + xh * N, N), c * 48:(c + 1) * 48, :].reshape(TOK, 128).astype(F32)
            xturn[c * 128:(c + 1) * 128, :] = x.T
        held[...] = xturn[pl.ds(pl.multiple_of(p * SF, 8), SF), :] * scale

    give(0, 2, 1, 3)
    give(1, 2, 0, 4)
    give(0, 2, 0, 3)
    give(1, 2, 1, 4)
    late_value = x_end(d_x, 1)
    rowdot = (late_value[1:2] * over_s - late_value[2:3] * over_t) / scale
    stacked = jnp.concatenate([scale, rowdot, jnp.zeros((126, TOK), F32)], axis=0)
    cols[...] = stacked.T
    for part in (0, 1):
        lo, hi = parts[part]
        near = g_own[7, lo:hi, :] + take(0, 1, part) + take(1, 1, part)
        g_own[0, lo:hi, :] = near + take(0, 2, part) + take(1, 2, part)

    give = g_own[0, pl.ds(pl.multiple_of((1 - xh) * SF, 8), SF), :]
    e_out[...] = jnp.concatenate([give, jnp.zeros((SP - SF, TOK), F32)], axis=0).astype(BF16)
    copy = remote(e_out, e_in, e_send.at[0], e_recv.at[0], across)
    copy.start()
    sent.append(copy)
    keep = g_own[0, pl.ds(pl.multiple_of(xh * SF, 8), SF), :]
    x_held = held[...]
    gains = gb[pl.ds(pl.multiple_of(v * SF, 8), SF), :]
    filler = jnp.zeros((128 - SF, 128), F32)
    gain_row = jnp.concatenate([gains, filler], axis=0).T[:ROWS]
    mycols = cols[pl.ds(pl.multiple_of((y * 2 + xl) * ROWS, 8), ROWS), :]
    my_scale, my_rowdot = mycols[:, 0:1], mycols[:, 1:2]
    copy.wait_recv()
    keep = keep + e_in[...].astype(F32)[:SF]
    gain_grad = jnp.sum(keep * x_held, axis=1, keepdims=True)
    gain_grad = jnp.concatenate([jnp.broadcast_to(gain_grad, (SF, 128)), filler], axis=0).T[:8]
    rough = gain_grad.astype(BF16).astype(F32)
    row = lax.broadcasted_iota(jnp.int32, (8, 128), 0)
    gain_grad = jnp.where(row == 0, rough, gain_grad - rough)
    keep = jnp.concatenate([keep, jnp.zeros((128 - SF, TOK), F32)], axis=0).T
    for m in range(2 * N):
        at = ((m % N) * 2 + m // N) * ROWS
        f_out[m] = jnp.concatenate([keep[at:at + ROWS], gain_grad], axis=0).astype(BF16)

    token_kl = late_value[0:1] / zt - jnp.log(zt) + jnp.log(zs)

    def final_send(m):
        return remote(f_out.at[m], f_in.at[slot], f_send.at[m], f_recv.at[slot], owner(m))

    def is_other(m):
        who = owner(m)
        return jnp.logical_not(jnp.logical_and(who[0] == d, who[1] == v))

    def send_final(i, _):
        m = (d + 1 + i) % (2 * N)

        @pl.when(is_other(m))
        def _():
            final_send(m).start()

        return 0

    lax.fori_loop(0, 2 * N, send_final, 0)

    loss_out[...] = jnp.sum(weight * token_kl, axis=1, keepdims=True)
    rest, split = token_kl, []
    for _ in range(3):
        split.append(rest.astype(BF16).astype(F32))
        rest = rest - split[-1]
    split = jnp.concatenate(split + [jnp.zeros((13, TOK), F32)], axis=0).astype(BF16)
    placed = dot_rows(split, perm[...])
    kl_out[...] = ((placed[0:1] + placed[1:2]) + placed[2:3]).reshape(TOK)

    @pl.when(self_in)
    def _():
        f_in[slot] = f_out[d]

    def wait_final(m, _):
        @pl.when(jnp.logical_not(jnp.logical_and(self_in, m == slot)))
        def _():
            remote(f_out.at[m], f_in.at[m], f_send.at[m], f_recv.at[m], sibling).wait_recv()

        return 0

    lax.fori_loop(0, 2 * N, wait_final, 0)
    got_all = f_in[0].astype(F32)
    for m in range(1, 2 * N):
        got_all = got_all + f_in[m].astype(F32)
    dnormed = got_all[:ROWS]
    x = pad_s[...]
    grad = gain_row * dnormed * my_scale - x * (my_scale**3 * my_rowdot / (SF * 4 * N))
    gh_out[...] = grad[:, :SF]
    gg_out[...] = (got_all[ROWS:ROWS + 1] + got_all[ROWS + 1:ROWS + 2])[:, :SF].reshape(SF)

    for copy in sent:
        copy.wait_send()

    def finish(m, _):
        @pl.when(is_other(m))
        def _():
            final_send(m).wait_send()

        return 0

    lax.fori_loop(0, 2 * N, finish, 0)


def outputs(kl, loss, gh, gg, kl_out, loss_out, gh_out, gg_out, sems):
    pairs = (kl, kl_out), (loss, loss_out), (gh, gh_out), (gg, gg_out)
    copies = [pltpu.make_async_copy(a, b, sems.at[i]) for i, (a, b) in enumerate(pairs)]
    for copy in copies:
        copy.start()
    for copy in copies:
        copy.wait()


def on_device(teacher_hidden, teacher_head, student_hidden, student_gain, student_head, token_mask):
    def shape(*dims):
        return jax.ShapeDtypeStruct(dims, F32)

    vmem = pl.BlockSpec(memory_space=pltpu.VMEM)
    anywhere = pl.BlockSpec(memory_space=pl.ANY)

    def half(*dims):
        return pltpu.VMEM(dims, BF16)

    def full(*dims):
        return pltpu.VMEM(dims, F32)

    dma = pltpu.SemaphoreType.DMA
    kl, loss, gh, gg = pl.pallas_call(
        body,
        out_shape=(shape(TOK), shape(1, 1), shape(ROWS, SF), shape(SF)),
        in_specs=[vmem, vmem, vmem, vmem, anywhere, anywhere],
        out_specs=(vmem, vmem, vmem, vmem),
        scratch_shapes=[
            half(4608, VOC), half(2304, VOC),
            half(4, VOC, 1152), half(VOC, 1152), half(2, VOC, 640), half(16, TF, VOC),
            full(2304, 128), full(2, 8, 640), half(TOK, TOK),
            full(ROWS, 256), full(ROWS, 128),
            half(2 * ROWS, 128), half(32, 2 * ROWS, 128),
            half(32, 3 * TF, 128), half(32, 3 * SP, 128),
            half(N, TF, TOK), half(2, TOK, 640), full(TOK, 128), full(TOK, 128),
            full(VOC, TOK), full(VOC, TOK), full(VOC, TOK), full(VOC, TOK),
            full(VOC, TOK), full(VOC, TOK), full(VOC, TOK), half(VOC, TOK),
            full(N, 2, TOK), full(N, 2, TOK), full(8, 2, TOK),
            full(N, 4, TOK), full(N, 4, TOK), full(8, 4, TOK),
            full(TOK, 128), full(640, TOK), full(SF, TOK),
            full(8, TF, TOK), half(8, TF, TOK), half(8, TF, TOK),
            half(8, TF, TOK), half(8, TF, TOK),
            half(SP, TOK), half(SP, TOK),
            half(16, 32, 128), half(16, 32, 128),
            dma((2,)), dma((31,)), dma((31,)),
            dma((64,)), dma((64,)), dma((32,)), dma((32,)),
            dma((16,)), dma((16,)), dma((16,)), dma((16,)), dma((14,)), dma((14,)),
            dma((8,)), dma((8,)), dma((16,)), dma((16,)), dma((1,)), dma((1,)), dma((16,)), dma((16,)),
        ],
        compiler_params=pltpu.CompilerParams(
            collective_id=0, has_side_effects=True, vmem_limit_bytes=56 * 1024 * 1024
        ),
        name="distill",
    )(
        teacher_hidden, student_hidden, student_gain.reshape(18, 128), token_mask,
        teacher_head, student_head,
    )
    kl, loss, gh, gg = pl.pallas_call(
        outputs,
        out_shape=(shape(TOK), shape(1, 1), shape(ROWS, SF), shape(SF)),
        in_specs=[anywhere] * 4,
        out_specs=(anywhere,) * 4,
        scratch_shapes=[dma((4,))],
        name="outputs",
    )(kl, loss, gh, gg)
    return kl, loss.reshape(()), gh, gg


def solution(mesh):
    placed = (
        P("dp", "vocab"),
        P(None, ("dp", "vocab")),
        P("dp", "vocab"),
        P(),
        P(None, ("dp", "vocab")),
        P(),
    )
    return jax.shard_map(
        on_device,
        mesh=mesh,
        in_specs=placed,
        out_specs=(P(), P(), P("dp", "vocab"), P("vocab")),
        check_vma=False,
    )
```

time: 92 us -> 87.8 us (0.954)
  the two profiles are of different devices: /device:TPU:8 before, /device:TPU:4 now
where the time goes in v3:
time: 87.8 us; the launch traced here: 87.7 us
  Pallas kernels  87 us (99%)
    pallas_call x1, Pallas kernels, on_device(): pl.pallas_call(body, out_shape=(shape(TOK), shape(1, 1), shape(ROWS, SF),...  84.8 us
    pallas_call x1, Pallas kernels, on_device(): pl.pallas_call(outputs, out_shape=(shape(TOK), shape(1, 1), shape(ROWS, S...  2.18 us

profile of v3, /device:TPU:4, one launch (start us, length us, event | category | flops | bytes accessed | tf_op | source)
XLA Modules:
  0.0 87.7 jit_solution(4616989150802571787)
XLA Ops:
  0.6 84.8 %distill.1 = (f32[384]{0:T(512)}, f32[1,1]{1,0:T(1,128)}, f32[24,72]{1,0:T(8,128)}, f32[72]{0:T(128)}) custom-call(bf16[24,144]{1,0:T(8,128)(2,1)} %th.1, bf16[24,72]{1,0:T(8,128)(2,1)} %sh.1, f32[18,128]{1,0:T(8,128)} %bitcast.2, s32[384]{0:T(512)} %mask.1, bf16[4608,256]{1,0:T(8,128)(2,1)} %wt_hbm.1, bf16[2304,256]{1,0:T(8,128)(2,1)} %ws_hbm.1), custom_call_target="tpu_custom_call" | custom-call | tf_op jit(solution)/shard_map/distill/pallas_call | solution.py:667
  85.5 2.2 %outputs.1 = (f32[384]{0:T(512)}, f32[1,1]{1,0:T(1,128)}, f32[24,72]{1,0:T(8,128)}, f32[72]{0:T(128)}) custom-call(f32[384]{0:T(512)} %get-tuple-element.12.kl, f32[1,1]{1,0:T(1,128)} %get-tuple-element.13.loss, f32[24,72]{1,0:T(8,128)} %get-tuple-element.14.gh, f32[72]{0:T(128)} %get-tuple-element.15.gg), custom_call_target="tpu_custom_call" | custom-call | tf_op jit(solution)/shard_map/outputs/pallas_call | solution.py:702

commit v4 on v3

--- a/solution.py
+++ b/solution.py
@@ -480,31 +480,35 @@
         remote(g_out.at[i], g_in.at[i], gs_send.at[i], gs_recv.at[i], sibling).wait_recv()
         g_own[i] = g_own[i] + g_in[i].astype(F32)
 
-    parts = (0, SP), (SP, 2 * SF)
-    right2, left2 = ring((p + 2) % N), ring((p + N - 2) % N)
-
-    def give(way, dist, part, i):
-        at, (lo, hi) = way * 4 + dist - 1, parts[part]
-        value = g_own[i, lo:hi, :]
+    spare = jnp.zeros((SP - SF, TOK), F32)
+
+    def keeper(half, place):
+        a = jnp.where(xh == half, xl, 1 - xl)
+        return dev(a, jnp.where(first, y, place), half, jnp.where(first, place, z), s)
+
+    def give(way, dist, half, i):
+        at = (way * 4 + dist - 1) * 2
+        value = g_own[i, half * SF:(half + 1) * SF, :]
         if dist == 2:
-            value = value + take(way, 3, part)
-            if part == way:
-                value = value + take(way, 4, part)
-        r_out[at, lo:hi, :] = value.astype(BF16)
-        to = ((right, left), (right2, left2))[dist in (2, 4)][way]
-        copy = remote(
-            r_out.at[at, lo:hi], r_in.at[at, lo:hi], rr_send.at[at * 2 + part], rr_recv.at[at * 2 + part], to
-        )
+            value = value + take(way, 3, half)
+            if half == way:
+                value = value + take(way, 4, half)
+        r_out[at + half] = jnp.concatenate([value, spare], axis=0).astype(BF16)
+        place = (p + (N - dist if way else dist)) % N
+        if dist != 2:
+            to, land = ((right, left), (right2, left2))[dist == 4][way], half
+        else:
+            to, land = keeper(half, place), jnp.where(xh == half, 0, 1)
+        copy = remote(r_out.at[at + half], r_in.at[at + land], rr_send.at[at + half], rr_recv.at[at + land], to)
         copy.start()
         sent.append(copy)
 
-    def take(way, dist, part):
-        at, (lo, hi) = way * 4 + dist - 1, parts[part]
-        remote(
-            r_out.at[at, lo:hi], r_in.at[at, lo:hi], rr_send.at[at * 2 + part], rr_recv.at[at * 2 + part], sibling
-        ).wait_recv()
-        return r_in[at, lo:hi, :].astype(F32)
-
+    def take(way, dist, land):
+        at = (way * 4 + dist - 1) * 2 + land
+        remote(r_out.at[at], r_in.at[at], rr_send.at[at], rr_recv.at[at], sibling).wait_recv()
+        return r_in[at].astype(F32)[:SF]
+
+    right2, left2 = ring((p + 2) % N), ring((p + N - 2) % N)
     chunk(0)
     chunk(1)
     chunk(2)
@@ -521,12 +525,12 @@
         chunk(i)
     own(5)
     own(6)
-    for part in (0, 1):
-        give(0, 1, part, 5)
-        give(1, 1, part, 6)
+    own(7)
+    for half in (0, 1):
+        give(0, 1, half, 5)
+        give(1, 1, half, 6)
     own(3)
     own(4)
-    own(7)
 
     late_value = line_end(d_y, y_send, y_recv, 1, y)
     x_start(d_x, 1, late_value)
@@ -545,29 +549,31 @@
     give(1, 2, 0, 4)
     give(0, 2, 0, 3)
     give(1, 2, 1, 4)
+    for half in (0, 1):
+        near = g_own[7, half * SF:(half + 1) * SF, :] + take(0, 1, half) + take(1, 1, half)
+        g_own[7, half * SF:(half + 1) * SF, :] = near
+    other = g_own[7, pl.ds(pl.multiple_of((1 - xh) * SF, 8), SF), :]
+    e_out[...] = jnp.concatenate([other, spare], axis=0).astype(BF16)
+    e_copy = remote(e_out, e_in, e_send.at[0], e_recv.at[0], across)
+    e_copy.start()
+    sent.append(e_copy)
+    keep = g_own[7, pl.ds(pl.multiple_of(xh * SF, 8), SF), :]
+    e_copy.wait_recv()
+    keep = keep + e_in[...].astype(F32)[:SF]
     late_value = x_end(d_x, 1)
     rowdot = (late_value[1:2] * over_s - late_value[2:3] * over_t) / scale
     stacked = jnp.concatenate([scale, rowdot, jnp.zeros((126, TOK), F32)], axis=0)
     cols[...] = stacked.T
-    for part in (0, 1):
-        lo, hi = parts[part]
-        near = g_own[7, lo:hi, :] + take(0, 1, part) + take(1, 1, part)
-        g_own[0, lo:hi, :] = near + take(0, 2, part) + take(1, 2, part)
-
-    give = g_own[0, pl.ds(pl.multiple_of((1 - xh) * SF, 8), SF), :]
-    e_out[...] = jnp.concatenate([give, jnp.zeros((SP - SF, TOK), F32)], axis=0).astype(BF16)
-    copy = remote(e_out, e_in, e_send.at[0], e_recv.at[0], across)
-    copy.start()
-    sent.append(copy)
-    keep = g_own[0, pl.ds(pl.multiple_of(xh * SF, 8), SF), :]
+    for land in (0, 1):
+        for way in (0, 1):
+            keep = keep + take(way, 2, land)
+
     x_held = held[...]
     gains = gb[pl.ds(pl.multiple_of(v * SF, 8), SF), :]
     filler = jnp.zeros((128 - SF, 128), F32)
     gain_row = jnp.concatenate([gains, filler], axis=0).T[:ROWS]
     mycols = cols[pl.ds(pl.multiple_of((y * 2 + xl) * ROWS, 8), ROWS), :]
     my_scale, my_rowdot = mycols[:, 0:1], mycols[:, 1:2]
-    copy.wait_recv()
-    keep = keep + e_in[...].astype(F32)[:SF]
     gain_grad = jnp.sum(keep * x_held, axis=1, keepdims=True)
     gain_grad = jnp.concatenate([jnp.broadcast_to(gain_grad, (SF, 128)), filler], axis=0).T[:8]
     rough = gain_grad.astype(BF16).astype(F32)
@@ -641,13 +647,11 @@
     lax.fori_loop(0, 2 * N, finish, 0)
 
 
-def outputs(kl, loss, gh, gg, kl_out, loss_out, gh_out, gg_out, sems):
-    pairs = (kl, kl_out), (loss, loss_out), (gh, gh_out), (gg, gg_out)
-    copies = [pltpu.make_async_copy(a, b, sems.at[i]) for i, (a, b) in enumerate(pairs)]
-    for copy in copies:
-        copy.start()
-    for copy in copies:
-        copy.wait()
+def outputs(kl, loss, gh, gg, kl_out, loss_out, gh_out, gg_out):
+    kl_out[...] = kl[...]
+    loss_out[...] = loss[...]
+    gh_out[...] = gh[...]
+    gg_out[...] = gg[...]
 
 
 def on_device(teacher_hidden, teacher_head, student_hidden, student_gain, student_head, token_mask):
@@ -683,7 +687,7 @@
             full(N, 4, TOK), full(N, 4, TOK), full(8, 4, TOK),
             full(TOK, 128), full(640, TOK), full(SF, TOK),
             full(8, TF, TOK), half(8, TF, TOK), half(8, TF, TOK),
-            half(8, TF, TOK), half(8, TF, TOK),
+            half(16, SP, TOK), half(16, SP, TOK),
             half(SP, TOK), half(SP, TOK),
             half(16, 32, 128), half(16, 32, 128),
             dma((2,)), dma((31,)), dma((31,)),
@@ -702,9 +706,8 @@
     kl, loss, gh, gg = pl.pallas_call(
         outputs,
         out_shape=(shape(TOK), shape(1, 1), shape(ROWS, SF), shape(SF)),
-        in_specs=[anywhere] * 4,
-        out_specs=(anywhere,) * 4,
-        scratch_shapes=[dma((4,))],
+        in_specs=[vmem] * 4,
+        out_specs=(vmem,) * 4,
         name="outputs",
     )(kl, loss, gh, gg)
     return kl, loss.reshape(()), gh, gg

time: 87.8 us -> 86 us (0.979)
  the two profiles are of different devices: /device:TPU:4 before, /device:TPU:8 now
where the time goes in v4:
time: 86 us; the launch traced here: 85.8 us
  Pallas kernels  85.1 us (99%)
    pallas_call x1, Pallas kernels, on_device(): pl.pallas_call(body, out_shape=(shape(TOK), shape(1, 1), shape(ROWS, SF),...  83.2 us
    pallas_call x1, Pallas kernels, on_device(): pl.pallas_call(outputs, out_shape=(shape(TOK), shape(1, 1), shape(ROWS, S...  1.93 us

profile of v4, /device:TPU:8, one launch (start us, length us, event | category | flops | bytes accessed | tf_op | source)
XLA Modules:
  0.0 85.8 jit_solution(3156927267125848895)
XLA Ops:
  0.6 83.2 %distill.1 = (f32[384]{0:T(512)}, f32[1,1]{1,0:T(1,128)}, f32[24,72]{1,0:T(8,128)}, f32[72]{0:T(128)}) custom-call(bf16[24,144]{1,0:T(8,128)(2,1)} %th.1, bf16[24,72]{1,0:T(8,128)(2,1)} %sh.1, f32[18,128]{1,0:T(8,128)} %bitcast.2, s32[384]{0:T(512)} %mask.1, bf16[4608,256]{1,0:T(8,128)(2,1)} %wt_hbm.1, bf16[2304,256]{1,0:T(8,128)(2,1)} %ws_hbm.1), custom_call_target="tpu_custom_call" | custom-call | tf_op jit(solution)/shard_map/distill/pallas_call | solution.py:671
  83.8 1.9 %outputs.1 = (f32[384]{0:T(512)}, f32[1,1]{1,0:T(1,128)}, f32[24,72]{1,0:T(8,128)}, f32[72]{0:T(128)}) custom-call(f32[384]{0:T(512)} %get-tuple-element.12.kl, f32[1,1]{1,0:T(1,128)} %get-tuple-element.13.loss, f32[24,72]{1,0:T(8,128)} %get-tuple-element.14.gh, f32[72]{0:T(128)} %get-tuple-element.15.gg), custom_call_target="tpu_custom_call" | custom-call | tf_op jit(solution)/shard_map/outputs/pallas_call | solution.py:706

commit v5 on v4

--- a/solution.py
+++ b/solution.py
@@ -86,6 +86,12 @@
     got[xh * 2 * N + slot] = piece[...]
     pl.semaphore_wait(barrier, len(line_mates) + 3)
     sent = []
+
+    def drain(count):
+        for copy in sent[:count]:
+            copy.wait_send()
+        del sent[:count]
+
 
     for i, mate in enumerate(line_mates):
         copy = remote(piece, got.at[xh * 2 * N + slot], p_send.at[i], p_recv.at[i], member(*mate))
@@ -360,9 +366,10 @@
     def student(i, carry):
         at = pl.ds(pl.multiple_of(i * step_rows, step_rows), step_rows)
         logit = ls[at, :]
-        pupil = 30.0 * jnp.tanh(logit / 30.0)
+        bent = jnp.tanh(logit * (1.0 / 30.0))
+        pupil = 30.0 * bent
         e = jnp.exp(pupil - 30.0)
-        slope = 1.0 - (pupil / 30.0) ** 2
+        slope = 1.0 - bent * bent
         pu[at, :], ep[at, :], qq[at, :] = pupil, e, slope
         sl = slope * logit
         ql[at, :] = sl
@@ -383,7 +390,7 @@
 
     def teacher(i, carry):
         at = pl.ds(pl.multiple_of(i * step_rows, step_rows), step_rows)
-        teach = 30.0 * jnp.tanh(lt[at, :] / 30.0)
+        teach = 30.0 * jnp.tanh(lt[at, :] * (1.0 / 30.0))
         e = jnp.exp(teach - 30.0)
         et[at, :] = e
         return (
@@ -442,12 +449,18 @@
     def along_y(t):
         return dev(xl, t, xh, z, s)
 
+    old = len(sent)
     line_start(s_z, z_send, z_recv, 0, z, along_z, main_sums)
+    drain(old)
     value = line_end(s_z, z_send, z_recv, 0, z)
+    old = len(sent)
     line_start(s_y, y_send, y_recv, 0, y, along_y, value)
     line_start(d_z, z_send, z_recv, 1, z, along_z, late_sums)
+    drain(old)
     value = line_end(s_y, y_send, y_recv, 0, y)
+    old = len(sent)
     x_start(s_x, 0, value)
+    drain(old)
     late_value = line_end(d_z, z_send, z_recv, 1, z)
     line_start(d_y, y_send, y_recv, 1, y, along_y, late_value)
     value = x_end(s_x, 0)
@@ -521,19 +534,24 @@
     give(1, 3, 0, 2)
     give(0, 3, 0, 1)
     give(1, 3, 1, 2)
-    for i in range(3, 8):
-        chunk(i)
+    chunk(5)
+    chunk(6)
+    chunk(3)
     own(5)
     own(6)
-    own(7)
     for half in (0, 1):
         give(0, 1, half, 5)
         give(1, 1, half, 6)
+    chunk(4)
+    chunk(7)
+    own(7)
     own(3)
     own(4)
 
     late_value = line_end(d_y, y_send, y_recv, 1, y)
+    old = len(sent) - 10
     x_start(d_x, 1, late_value)
+    drain(old)
     @pl.when(first)
     def _():
         held[...] = features_first(xh * N + p) * scale
@@ -586,23 +604,20 @@
 
     token_kl = late_value[0:1] / zt - jnp.log(zt) + jnp.log(zs)
 
-    def final_send(m):
-        return remote(f_out.at[m], f_in.at[slot], f_send.at[m], f_recv.at[slot], owner(m))
-
-    def is_other(m):
-        who = owner(m)
-        return jnp.logical_not(jnp.logical_and(who[0] == d, who[1] == v))
-
-    def send_final(i, _):
-        m = (d + 1 + i) % (2 * N)
-
-        @pl.when(is_other(m))
-        def _():
-            final_send(m).start()
-
-        return 0
-
-    lax.fori_loop(0, 2 * N, send_final, 0)
+    def final_send(i, da, dj):
+        a, j = xl ^ da, (y + dj) % N
+        return remote(f_out.at[a * N + j], f_in.at[slot], f_send.at[i], f_recv.at[slot], owner(a * N + j))
+
+    ways = [(da, dj) for dj in far_first + (0,) for da in (1, 0) if da or dj]
+    old = len(sent)
+    for i, way in enumerate(ways):
+        copy = final_send(i, *way)
+        copy.start()
+        sent.append(copy)
+
+    @pl.when(jnp.logical_not(self_in))
+    def _():
+        final_send(15, 0, 0).start()
 
     loss_out[...] = jnp.sum(weight * token_kl, axis=1, keepdims=True)
     rest, split = token_kl, []
@@ -616,6 +631,8 @@
     @pl.when(self_in)
     def _():
         f_in[slot] = f_out[d]
+
+    drain(old)
 
     def wait_final(m, _):
         @pl.when(jnp.logical_not(jnp.logical_and(self_in, m == slot)))
@@ -634,17 +651,11 @@
     gh_out[...] = grad[:, :SF]
     gg_out[...] = (got_all[ROWS:ROWS + 1] + got_all[ROWS + 1:ROWS + 2])[:, :SF].reshape(SF)
 
-    for copy in sent:
-        copy.wait_send()
-
-    def finish(m, _):
-        @pl.when(is_other(m))
-        def _():
-            final_send(m).wait_send()
-
-        return 0
-
-    lax.fori_loop(0, 2 * N, finish, 0)
+    drain(len(sent))
+
+    @pl.when(jnp.logical_not(self_in))
+    def _():
+        final_send(15, 0, 0).wait_send()
 
 
 def outputs(kl, loss, gh, gg, kl_out, loss_out, gh_out, gg_out):

time: 86 us -> 85.8 us (level)
  the two profiles are of different devices: /device:TPU:8 before, /device:TPU:13 now
where the time goes in v5:
time: 85.8 us; the launch traced here: 85.5 us
  Pallas kernels  84.9 us (99%)
    pallas_call x1, Pallas kernels, on_device(): pl.pallas_call(body, out_shape=(shape(TOK), shape(1, 1), shape(ROWS, SF),...  83 us
    pallas_call x1, Pallas kernels, on_device(): pl.pallas_call(outputs, out_shape=(shape(TOK), shape(1, 1), shape(ROWS, S...  1.93 us

profile of v5, /device:TPU:13, one launch (start us, length us, event | category | flops | bytes accessed | tf_op | source)
XLA Modules:
  0.0 85.5 jit_solution(16752363210050673260)
XLA Ops:
  0.6 83.0 %distill.1 = (f32[384]{0:T(512)}, f32[1,1]{1,0:T(1,128)}, f32[24,72]{1,0:T(8,128)}, f32[72]{0:T(128)}) custom-call(bf16[24,144]{1,0:T(8,128)(2,1)} %th.1, bf16[24,72]{1,0:T(8,128)(2,1)} %sh.1, f32[18,128]{1,0:T(8,128)} %bitcast.2, s32[384]{0:T(512)} %mask.1, bf16[4608,256]{1,0:T(8,128)(2,1)} %wt_hbm.1, bf16[2304,256]{1,0:T(8,128)(2,1)} %ws_hbm.1), custom_call_target="tpu_custom_call" | custom-call | tf_op jit(solution)/shard_map/distill/pallas_call | solution.py:682
  83.6 1.9 %outputs.1 = (f32[384]{0:T(512)}, f32[1,1]{1,0:T(1,128)}, f32[24,72]{1,0:T(8,128)}, f32[72]{0:T(128)}) custom-call(f32[384]{0:T(512)} %get-tuple-element.12.kl, f32[1,1]{1,0:T(1,128)} %get-tuple-element.13.loss, f32[24,72]{1,0:T(8,128)} %get-tuple-element.14.gh, f32[72]{0:T(128)} %get-tuple-element.15.gg), custom_call_target="tpu_custom_call" | custom-call | tf_op jit(solution)/shard_map/outputs/pallas_call | solution.py:717
